TPU v7x, 32 devices: a whole 2x2x4 slice. The times are simulated.
32 devices in a mesh: tile: 16 (over z, y, x), frame: 2 (over core).
Axes of the slice: x: 2, y: 2, z: 4, core: 2. Of those that a mesh axis runs over, the one named last changes fastest.
Arguments:
- latents: bfloat16 [64, 2, 104, 384], P('tile', 'frame'), may hold values from -80 to 80
- row_video: int32 [64], replicated, may hold values from 0 to 1, never falling along the last dimension, each value on 1 to 48 neighbouring positions
- video_cols: int32 [2], replicated, may hold values from 52 to 104, as said below
- first_gain: float32 [384], replicated, may hold values from 0.5 to 1.5
- first_shift: float32 [384], replicated, may hold values from -3 to 3
- conv_weight: bfloat16 [3, 3, 3, 384, 384], replicated, may hold values from -0.0625 to 0.0625
- conv_bias: float32 [384], replicated, may hold values from -3 to 3
- second_gain: float32 [384], replicated, may hold values from 0.5 to 1.5
- second_shift: float32 [384], replicated, may hold values from -3 to 3
- triple_weight: bfloat16 [384, 1152], replicated, may hold values from -0.55 to 0.55
- triple_bias: float32 [1152], replicated, may hold values from -3 to 3
- output_weight: bfloat16 [384, 384], replicated, may hold values from -0.3125 to 0.3125
- output_bias: float32 [384], replicated, may hold values from -3 to 3
- upsample_weight: bfloat16 [3, 3, 384, 192], replicated, may hold values from -0.109375 to 0.109375
- upsample_bias: float32 [192], replicated, may hold values from -3 to 3
Outputs:
- decoded: bfloat16 [128, 2, 208, 192], P('tile', 'frame')
Inputs may be any that keep to these rules, and one draw needn't show every extreme that they name: `row_video`: video numbers never fall along the rows; every video has 1 to 48 rows. `video_cols`: one video has all 104 columns.
All inputs are finite; a program needn't handle non-finite values.
Results may differ from a plain program's by a relative error of at most 0.013.
The roundings to bfloat16 on the way count: a program that leaves them out, or rounds other values in their place, can miss the bound.
Values may be sent and summed in bfloat16 or wider, within the bound.
No kernel may reach another device: no remote copies, remote signals or barrier semaphores. Data moves between devices by JAX's collectives and lax.ppermute only.
A program may use at most 128 MiB of HBM per device.

v0:
```python
import jax
import jax.numpy as jnp
from jax import lax
from jax.sharding import PartitionSpec as P

GROUPS = 32


EPSILON = 1e-05
MASKED = -1e30
HIGHEST = lax.Precision.HIGHEST


def shifted(shard, axis, by):
    length = lax.axis_size(axis)
    pairs = [(i, i + by) for i in range(length) if 0 <= i + by < length]
    return lax.ppermute(shard, axis, pairs)


def padded_2(shard, sides, width):
    for axis, dim in sides:
        size, length = (lax.axis_size(axis), shard.shape[dim])
        up = [(i, (i + 1) % size) for i in range(size - 1)]
        down = [(j, i) for i, j in up]
        last = lax.slice_in_dim(shard, length - width, length, axis=dim)
        leading = lax.slice_in_dim(shard, 0, width, axis=dim)
        before = lax.ppermute(last, axis, up)
        after = lax.ppermute(leading, axis, down)
        shard = jnp.concatenate([before, shard, after], axis=dim)
    return shard


def video_lookup(labels, video_cols):
    numbers = jnp.arange(video_cols.shape[0], dtype=jnp.int32)
    matches = labels[:, None] == numbers[None, :]
    widths = jnp.sum(jnp.where(matches, video_cols[None, :], 0), axis=1)
    return (matches.astype(jnp.float32), widths)


def group_norm(values, norm_gain, norm_shift, onehot, valid_mask, counts):
    channels = values.shape[3]
    per_group = channels // GROUPS
    member = (
        jnp.arange(channels, dtype=jnp.int32)[:, None] // per_group
        == jnp.arange(GROUPS, dtype=jnp.int32)[None, :]
    ).astype(jnp.float32)
    mask_four = valid_mask.astype(jnp.float32)[:, None, :, None]
    masked = values * mask_four
    partial_sum = jnp.einsum("rfwc,cg,rv->fvg", masked, member, onehot, precision=HIGHEST)
    group_mean = lax.psum(partial_sum, "tile") / counts
    mean_full = jnp.einsum("fvg,rv,cg->rfc", group_mean, onehot, member, precision=HIGHEST)
    centered = (values - mean_full[:, :, None, :]) * mask_four
    partial_spread = jnp.einsum(
        "rfwc,cg,rv->fvg", centered * centered, member, onehot, precision=HIGHEST
    )
    variance = lax.psum(partial_spread, "tile") / counts
    scale_full = jnp.einsum(
        "fvg,rv,cg->rfc", lax.rsqrt(variance + EPSILON), onehot, member, precision=HIGHEST
    )
    return centered * scale_full[:, :, None, :] * norm_gain + norm_shift


def causal_context(hidden):
    earlier = shifted(hidden, "frame", 1)
    farther = shifted(hidden, "frame", 2)
    earlier = jnp.concatenate([farther, earlier], axis=1)
    stacked = jnp.concatenate([earlier, hidden], axis=1)
    context = padded_2(stacked, (("tile", 0),), 1)
    return context


def conv_taps(context, conv_weight, near_labels, own_labels):
    row_count = own_labels.shape[0]
    frame_count = context.shape[1] - 2
    col_count = context.shape[2]
    channels = context.shape[3]
    padded = jnp.pad(context, ((0, 0), (0, 0), (1, 1), (0, 0)))
    total = jnp.zeros((row_count * frame_count * col_count, conv_weight.shape[-1]), jnp.float32)
    for row_tap in range(3):
        same = (near_labels[row_tap : row_tap + row_count] == own_labels).astype(context.dtype)[
            :, None, None, None
        ]
        for time_tap in range(3):
            window = padded[row_tap : row_tap + row_count, time_tap : time_tap + frame_count] * same
            columns = jnp.concatenate(
                [window[:, :, col_tap : col_tap + col_count] for col_tap in range(3)], axis=-1
            )
            total = total + jnp.dot(
                columns.reshape(-1, 3 * channels),
                conv_weight[time_tap, row_tap].reshape(3 * channels, -1),
                preferred_element_type=jnp.float32,
            )
    return total.reshape(row_count, frame_count, col_count, -1)


def upsample_conv(rimmed, weight, near_labels, own_labels):
    row_count = own_labels.shape[0]
    frame_count = rimmed.shape[1]
    wide_count = 2 * rimmed.shape[2]
    channels = rimmed.shape[3]
    doubled = jnp.repeat(jnp.repeat(rimmed, 2, axis=0), 2, axis=2)[1 : 2 * row_count + 3]
    doubled = jnp.pad(doubled, ((0, 0), (0, 0), (1, 1), (0, 0)))
    up_labels = jnp.repeat(near_labels, 2)[1 : 2 * row_count + 3]
    target_labels = jnp.repeat(own_labels, 2)
    total = jnp.zeros((2 * row_count * frame_count * wide_count, weight.shape[-1]), jnp.float32)
    for row_tap in range(3):
        same = (up_labels[row_tap : row_tap + 2 * row_count] == target_labels).astype(rimmed.dtype)[
            :, None, None, None
        ]
        window = doubled[row_tap : row_tap + 2 * row_count] * same
        columns = jnp.concatenate(
            [window[:, :, col_tap : col_tap + wide_count] for col_tap in range(3)], axis=-1
        )
        total = total + jnp.dot(
            columns.reshape(-1, 3 * channels),
            weight[row_tap].reshape(3 * channels, -1),
            preferred_element_type=jnp.float32,
        )
    return total.reshape(2 * row_count, frame_count, wide_count, -1)


def shards(
    latents,
    row_video,
    video_cols,
    first_gain,
    first_shift,
    conv_weight,
    conv_bias,
    second_gain,
    second_shift,
    triple_weight,
    triple_bias,
    output_weight,
    output_bias,
    upsample_weight,
    upsample_bias,
):
    row_count, frame_count, col_count, channels = latents.shape
    first_row = lax.axis_index("tile") * row_count
    canvas_onehot, canvas_widths = video_lookup(row_video, video_cols)
    counts = (
        jnp.sum(canvas_onehot, axis=0) * video_cols.astype(jnp.float32) * (channels // GROUPS)
    )[None, :, None]
    bordered = jnp.pad(row_video, 1, constant_values=-1)
    near_labels = lax.dynamic_slice_in_dim(bordered, first_row, row_count + 2)
    own_labels = near_labels[1 : row_count + 1]
    onehot, own_widths = video_lookup(own_labels, video_cols)
    column_ids = jnp.arange(col_count, dtype=jnp.int32)
    valid_mask = column_ids[None, :] < own_widths[:, None]
    mask_four = valid_mask[:, None, :, None]
    source = latents.astype(jnp.float32)
    first_normed = group_norm(source, first_gain, first_shift, onehot, valid_mask, counts)
    hidden = jnp.where(mask_four, jax.nn.silu(first_normed), 0.0).astype(jnp.bfloat16)
    context = causal_context(hidden)
    branch = conv_taps(context, conv_weight, near_labels, own_labels)
    after_conv = jnp.where(mask_four, source + branch + conv_bias, 0.0).astype(jnp.bfloat16)
    second_normed = jnp.where(
        mask_four,
        group_norm(
            after_conv.astype(jnp.float32), second_gain, second_shift, onehot, valid_mask, counts
        ),
        0.0,
    ).astype(jnp.bfloat16)
    flat_normed = second_normed.reshape(-1, channels)
    scale = channels ** (-0.5)
    lowest = own_labels[0]
    highest = own_labels[row_count - 1]
    block_rows = row_count
    while block_rows * col_count < 1024:
        block_rows = block_rows * 2

    def split_pairs(block):
        return (block[..., :channels], block[..., channels:])

    def attend_block(state, block, block_first, project, queries):
        rows_here = block.shape[0]
        block_labels = lax.dynamic_slice_in_dim(row_video, block_first, rows_here)
        block_widths = lax.dynamic_slice_in_dim(canvas_widths, block_first, rows_here)

        def update(carried):
            running_max, running_total, accum = carried
            key_block, value_block = project(block)
            key_flat = jnp.moveaxis(key_block, 1, 0).reshape(frame_count, -1, channels)
            value_flat = jnp.moveaxis(value_block, 1, 0).reshape(frame_count, -1, channels)
            scores = (
                jnp.einsum("rfwc,fkc->rfwk", queries, key_flat, preferred_element_type=jnp.float32)
                * scale
            )
            same_video = own_labels[:, None] == block_labels[None, :]
            key_valid = column_ids[None, :] < block_widths[:, None]
            allowed = (same_video[:, :, None] & key_valid[None, :, :]).reshape(row_count, -1)[
                :, None, None, :
            ]
            scores = jnp.where(allowed, scores, MASKED)
            new_max = jnp.maximum(running_max, jnp.max(scores, axis=3))
            weights = jnp.where(allowed, jnp.exp(scores - new_max[..., None]), 0.0)
            factor = jnp.exp(running_max - new_max)
            running_total = running_total * factor + jnp.sum(weights, axis=3)
            accum = accum * factor[..., None] + jnp.einsum(
                "rfwk,fkc->rfwc",
                weights.astype(jnp.bfloat16),
                value_flat,
                preferred_element_type=jnp.float32,
            )
            return (new_max, running_total, accum)

        def unchanged(carried):
            return carried

        touches = (block_labels[rows_here - 1] >= lowest) & (block_labels[0] <= highest)
        return lax.cond(touches, update, unchanged, state)

    initial = (
        jnp.full((row_count, frame_count, col_count), MASKED, jnp.float32),
        jnp.zeros((row_count, frame_count, col_count), jnp.float32),
        jnp.zeros((row_count, frame_count, col_count, channels), jnp.float32),
    )
    triple = (
        jnp.dot(flat_normed, triple_weight, preferred_element_type=jnp.float32) + triple_bias
    ).astype(jnp.bfloat16)
    triple = triple.reshape(row_count, frame_count, col_count, 3 * channels)
    queries = triple[..., :channels]
    shard_piece = lax.all_gather(triple[..., channels:], "tile", axis=0, tiled=True)
    piece_rows = shard_piece.shape[0]
    step_rows = block_rows

    def advance(position, carried):
        offset = position * step_rows
        block = lax.dynamic_slice_in_dim(shard_piece, offset, step_rows)
        return attend_block(carried, block, offset, split_pairs, queries)

    folded = lax.fori_loop(0, piece_rows // step_rows, advance, initial)
    running_max, running_total, accum = folded
    mixed = (accum / running_total[..., None]).astype(jnp.bfloat16)
    attended = jnp.dot(
        mixed.reshape(-1, channels), output_weight, preferred_element_type=jnp.float32
    ).reshape(row_count, frame_count, col_count, channels)
    after_attention = jnp.where(
        mask_four, after_conv.astype(jnp.float32) + attended + output_bias, 0.0
    ).astype(jnp.bfloat16)
    rimmed = padded_2(after_attention, (("tile", 0),), 1)
    decoded = upsample_conv(rimmed, upsample_weight, near_labels, own_labels)
    up_valid = (
        jnp.arange(2 * col_count, dtype=jnp.int32)[None, :] < 2 * jnp.repeat(own_widths, 2)[:, None]
    )
    return jnp.where(up_valid[:, None, :, None], decoded + upsample_bias, 0.0).astype(jnp.bfloat16)


def solution(mesh):
    in_specs = (
        P("tile", "frame", None, None),
        P(),
        P(),
        P(),
        P(),
        P(),
        P(),
        P(),
        P(),
        P(),
        P(),
        P(),
        P(),
        P(),
        P(),
    )
    out_specs = P("tile", "frame", None, None)
    return jax.shard_map(shards, mesh=mesh, in_specs=in_specs, out_specs=out_specs, check_vma=False)
```

profile of v0, /device:TPU:8, one launch (start us, length us, event | category | flops | bytes accessed | tf_op | source)
XLA Modules:
  0.0 402.1 jit_solution(13835290990604362556)
XLA Ops:
  10.8 35.6 %psum.28 = f32[1,2,32]{2,1,0:T(2,128)S(1)} all-reduce(f32[1,2,32]{2,1,0:T(2,128)S(1)} %convolution_bitcast_fusion.8), channel_id=1, replica_groups=mesh['tile'=16,'frame'=2] {'tile'}, use_global_device_ids=true, to_apply=%region_2.3 | all-reduce | flops 64 | bytes 512 | tf_op jit(solution)/shard_map/psum | solution.py:50
  49.2 36.6 %psum.29 = f32[1,2,32]{2,1,0:T(2,128)S(1)} all-reduce(f32[1,2,32]{2,1,0:T(2,128)S(1)} %convolution_bitcast_fusion.7), channel_id=1, replica_groups=mesh['tile'=16,'frame'=2] {'tile'}, use_global_device_ids=true, to_apply=%region_5.6 | all-reduce | flops 64 | bytes 512 | tf_op jit(solution)/shard_map/psum | solution.py:56
  90.9 3.9 collective-permute-start.2
  94.8 5.5 %collective-permute-start.3 = (bf16[1,3,104,384]{3,2,0,1:T(8,128)(2,1)S(1)}, bf16[1,3,104,384]{3,2,0,1:T(8,128)(2,1)S(1)}, u32[]{:S(2)}, u32[]{:S(2)}) collective-permute-start(bf16[1,3,104,384]{3,2,0,1:T(8,128)(2,1)S(1)} %get-tuple-element.418), channel_id=1, source_target_pairs={{2,0},{4,2},{6,4},{8,6},{10,8},{12,10},{14,12},{16,14},{18,16},{20... | collective-permute-start | bytes 718856 | tf_op jit(solution)/shard_map/ppermute | solution.py:28
  100.4 3.9 fusion.113
  117.5 38.3 %psum.30 = f32[1,2,32]{2,1,0:T(2,128)S(1)} all-reduce(f32[1,2,32]{2,1,0:T(2,128)S(1)} %convolution_bitcast_fusion.6), channel_id=1, replica_groups=mesh['tile'=16,'frame'=2] {'tile'}, use_global_device_ids=true, to_apply=%region_7.8 | all-reduce | flops 64 | bytes 512 | tf_op jit(solution)/shard_map/psum | solution.py:50
  157.0 37.0 %psum.31 = f32[1,2,32]{2,1,0:T(2,128)S(1)} all-reduce(f32[1,2,32]{2,1,0:T(2,128)S(1)} %convolution_bitcast_fusion.5), channel_id=1, replica_groups=mesh['tile'=16,'frame'=2] {'tile'}, use_global_device_ids=true, to_apply=%region_9.10 | all-reduce | flops 64 | bytes 512 | tf_op jit(solution)/shard_map/psum | solution.py:56
  199.7 129.7 %all-gather.2.cloned.1.call-done = bf16[64,1,104,768]{3,2,1,0:T(8,128)(2,1)} async-done(((bf16[4,1,104,768]{3,2,1,0:T(8,128)(2,1)}), bf16[64,1,104,768]{3,2,1,0:T(8,128)(2,1)}) %all-gather.2.cloned.1.call-update) | async-done | bytes 10223632 | tf_op jit(solution)/shard_map/all_gather | solution.py:224
  329.5 23.8 %while.18 = (s32[]{:T(128)}, f32[4,1,104]{2,0,1:T(4,128)S(1)}, f32[4,1,104]{2,0,1:T(4,128)S(1)}, f32[4,1,104,384]{3,2,0,1:T(8,128)S(1)}, s32[64]{0:T(128)S(1)}, ...) while((s32[]{:T(128)}, f32[4,1,104]{2,0,1:T(4,128)S(1)}, ...), condition=%wide.region_16.17_spmd.clone, body=%wide.region_11.16_spmd.clone.sunk | while | flops 1069815168 | bytes 17710040 | solution.py:233
  332.6 5.6 %conditional.3 = ((f32[4,1,104]{2,0,1:T(4,128)S(1)}, f32[4,1,104]{2,0,1:T(4,128)S(1)}, f32[4,1,104,384]{3,2,0,1:T(8,128)S(1)})) conditional(s32[]{:T(128)} %convert_element_type.177, (f32[4,1,104]{2,0,1:T(4,128)S(1)}, f32[4,1,104]{2,0,1:T(4,128)S(1)}, f32[4,1,104,384]{3,2,0,1:T(8,128)S(1)}) %tuple.111, (s32[4]{0:T(128)S(1)}, s32[16]{0:T(128)S(1)}, ...), branch_computations={%region_12.12_spmd, %region_13.15_spmd} | conditional | flops 1069815168 | bytes 17709160 | solution.py:212
  333.3 2.0 constant_dynamic-slice_fusion.1
  341.4 5.6 %conditional.3 = ((f32[4,1,104]{2,0,1:T(4,128)S(1)}, f32[4,1,104]{2,0,1:T(4,128)S(1)}, f32[4,1,104,384]{3,2,0,1:T(8,128)S(1)})) conditional(s32[]{:T(128)} %convert_element_type.177, (f32[4,1,104]{2,0,1:T(4,128)S(1)}, f32[4,1,104]{2,0,1:T(4,128)S(1)}, f32[4,1,104,384]{3,2,0,1:T(8,128)S(1)}) %tuple.111, (s32[4]{0:T(128)S(1)}, s32[16]{0:T(128)S(1)}, ...), branch_computations={%region_12.12_spmd, %region_13.15_spmd} | conditional | flops 1069815168 | bytes 17709160 | solution.py:212
  342.1 2.0 constant_dynamic-slice_fusion.1
  353.8 3.4 collective-permute-start.4
  357.2 4.3 %collective-permute-start.5 = (bf16[1,1,104,384]{3,2,0,1:T(8,128)(2,1)S(1)}, bf16[1,1,104,384]{3,2,0,1:T(8,128)(2,1)}, u32[]{:S(2)}, u32[]{:S(2)}) collective-permute-start(bf16[1,1,104,384]{3,2,0,1:T(8,128)(2,1)S(1)} %get-tuple-element.438), channel_id=1, source_target_pairs={{2,0},{4,2},{6,4},{8,6},{10,8},{12,10},{14,12},{16,14},{18,16},{20... | collective-permute-start | bytes 239624 | tf_op jit(solution)/shard_map/ppermute | solution.py:28
  364.4 1.4 concatenate.69
  365.7 8.5 %collective-permute-done.5 = bf16[1,1,104,384]{3,2,0,1:T(8,128)(2,1)} collective-permute-done((bf16[1,1,104,384]{3,2,0,1:T(8,128)(2,1)S(1)}, bf16[1,1,104,384]{3,2,0,1:T(8,128)(2,1)}, u32[]{:S(2)}, u32[]{:S(2)}) %collective-permute-start.5) | collective-permute-done | bytes 79904 | tf_op jit(solution)/shard_map/ppermute | solution.py:28
  375.4 2.0 broadcast_in_dim.169
  377.4 3.7 broadcast_in_dim.170
  385.8 1.4 fusion.21
  387.2 1.4 convolution_add_fusion.2
  388.6 1.4 convolution_add_fusion.1
  390.1 2.3 reshape.453
  392.3 2.9 fusion.30
  (178 shorter events, 50.9 us)
Async XLA Ops:
  6.5 188.2 %copy-start = (bf16[384,1152]{1,0:T(8,128)(2,1)S(1)}, bf16[384,1152]{1,0:T(8,128)(2,1)}, u32[]{:S(2)}) copy-start(bf16[384,1152]{1,0:T(8,128)(2,1)} %param.28) | copy-start | bytes 2654212
  6.5 322.9 %all-gather.2.cloned.1.call-start = ((), (), s32[]{:S(2)}) async-start(), calls=%async_computation | async-start | bytes 10862592 | tf_op jit(solution)/shard_map/all_gather | solution.py:224
  87.6 2.0 collective-permute-start
  88.3 2.5 collective-permute-start.1
  90.9 14.7 %collective-permute-start.2 = (bf16[1,3,104,384]{3,2,0,1:T(8,128)(2,1)S(1)}, bf16[1,3,104,384]{3,2,0,1:T(8,128)(2,1)S(1)}, u32[]{:S(2)}, u32[]{:S(2)}) collective-permute-start(bf16[1,3,104,384]{3,2,0,1:T(8,128)(2,1)S(1)} %get-tuple-element.417), channel_id=1, source_target_pairs={{0,2},{2,4},{4,6},{6,8},{8,10},{10,12},{12,14},{14,16},{16,18},{18... | collective-permute-start | bytes 718856 | tf_op jit(solution)/shard_map/ppermute | solution.py:27
  94.8 11.5 %collective-permute-start.3 = (bf16[1,3,104,384]{3,2,0,1:T(8,128)(2,1)S(1)}, bf16[1,3,104,384]{3,2,0,1:T(8,128)(2,1)S(1)}, u32[]{:S(2)}, u32[]{:S(2)}) collective-permute-start(bf16[1,3,104,384]{3,2,0,1:T(8,128)(2,1)S(1)} %get-tuple-element.418), channel_id=1, source_target_pairs={{2,0},{4,2},{6,4},{8,6},{10,8},{12,10},{14,12},{16,14},{18,16},{20... | collective-permute-start | bytes 718856 | tf_op jit(solution)/shard_map/ppermute | solution.py:28
  115.7 1.0 copy-start.2
  115.8 1.0 copy-start.7
  115.8 78.7 %copy-start.8 = (f32[384]{0:T(512)S(1)}, f32[384]{0:T(512)}, u32[]{:S(2)}) copy-start(f32[384]{0:T(512)} %param.27) | copy-start | bytes 4612
  115.8 78.7 %copy-start.9 = (f32[384]{0:T(512)S(1)}, f32[384]{0:T(512)}, u32[]{:S(2)}) copy-start(f32[384]{0:T(512)} %param.26) | copy-start | bytes 4612
  116.5 78.2 %copy-start.12 = (f32[1152]{0:T(1024)S(1)}, f32[1152]{0:T(1024)}, u32[]{:S(2)}) copy-start(f32[1152]{0:T(1024)} %param.29) | copy-start | bytes 13828
  194.7 3.7 copy-start.14
  194.7 3.7 copy-start.15
  194.8 3.8 copy-start.3
  195.5 0.9 copy-start.5
  329.5 23.8 %copy-start.11 = (bf16[384,384]{1,0:T(8,128)(2,1)S(1)}, bf16[384,384]{1,0:T(8,128)(2,1)}, u32[]{:S(2)}) copy-start(bf16[384,384]{1,0:T(8,128)(2,1)} %param.30) | copy-start | bytes 884740
  329.5 23.8 %copy-start.13 = (f32[384]{0:T(512)S(1)}, f32[384]{0:T(512)}, u32[]{:S(2)}) copy-start(f32[384]{0:T(512)} %param.31) | copy-start | bytes 4612
  353.8 11.9 %collective-permute-start.4 = (bf16[1,1,104,384]{3,2,0,1:T(8,128)(2,1)S(1)}, bf16[1,1,104,384]{3,2,0,1:T(8,128)(2,1)S(1)}, u32[]{:S(2)}, u32[]{:S(2)}) collective-permute-start(bf16[1,1,104,384]{3,2,0,1:T(8,128)(2,1)S(1)} %get-tuple-element.437), channel_id=1, source_target_pairs={{0,2},{2,4},{4,6},{6,8},{8,10},{10,12},{12,14},{14,16},{16,18},{18... | collective-permute-start | bytes 239624 | tf_op jit(solution)/shard_map/ppermute | solution.py:27
  357.2 17.1 %collective-permute-start.5 = (bf16[1,1,104,384]{3,2,0,1:T(8,128)(2,1)S(1)}, bf16[1,1,104,384]{3,2,0,1:T(8,128)(2,1)}, u32[]{:S(2)}, u32[]{:S(2)}) collective-permute-start(bf16[1,1,104,384]{3,2,0,1:T(8,128)(2,1)S(1)} %get-tuple-element.438), channel_id=1, source_target_pairs={{2,0},{4,2},{6,4},{8,6},{10,8},{12,10},{14,12},{16,14},{18,16},{20... | collective-permute-start | bytes 239624 | tf_op jit(solution)/shard_map/ppermute | solution.py:28
  384.4 1.3 copy-start.4
  384.4 1.4 copy-start.6
  388.6 6.6 %copy-start.1 = (bf16[384,1152]{1,0:T(8,128)(2,1)S(1)}, bf16[384,1152]{1,0:T(8,128)(2,1)}, u32[]{:S(2)}) copy-start(bf16[384,1152]{1,0:T(8,128)(2,1)} %param.28) | copy-start | bytes 2654212
  390.0 2.3 copy-start.10
Sparse Core Ops, SparseCore 0:
  197.4 131.9 all-gather.1
where the time goes:
time: 404 us; the launch traced here: 402 us
  blocking collectives  147 us (36%)
  waiting for transfers between devices  141 us (35%)
  local copies, waits for them, and re-layouts  33.5 us (8%)
  matrix products  20.2 us (5%)
  starting transfers between devices  19.1 us (5%)
  other arithmetic  16.3 us (4%)
  between operations  14 us (3%)
  loops' own time  10.1 us (2%)
    all_gather x1, waiting for transfers between devices, shards(): lax.all_gather(triple[..., channels:], 'tile', axis=0, tiled=True)  130 us
    psum x2, blocking collectives, group_norm(): group_mean = lax.psum(partial_sum, 'tile') / counts  73.9 us
    psum x2, blocking collectives, group_norm(): variance = lax.psum(partial_spread, 'tile') / counts  73.6 us
    another operation x1, loops' own time, shards(): folded = lax.fori_loop(0, piece_rows // step_rows, advance, initial)  9.9 us
    ppermute x2, starting transfers between devices, padded_2(): after = lax.ppermute(leading, axis, down)  9.8 us
    ppermute x2, waiting for transfers between devices, padded_2(): after = lax.ppermute(leading, axis, down)  9.26 us
  transfers between devices with their start and end apart: 7, of which 5 were waited for; matrix products, arithmetic and copies ran while one was open for 3% of the time, Pallas kernels for 0%

commit v1 on v0

v1 whole, which is shorter than its diff:
```python
import functools
import math

import jax
import jax.numpy as jnp
from jax import lax
from jax.experimental import pallas as pl
from jax.experimental.pallas import tpu as pltpu
from jax.sharding import PartitionSpec as P

GROUPS = 32
EPSILON = 1e-05
MASKED = -1e30
LOWEST = -5e29
HIGHEST = lax.Precision.HIGHEST
BOTH = ("tile", "frame")
SLOTS = 8
LANES = 128
KEY_BLOCK = 512
VMEM_BYTES = 40 * 1024 * 1024
F32 = jnp.float32
BF16 = jnp.bfloat16

SMEM_SPEC = pl.BlockSpec(memory_space=pltpu.SMEM)
VMEM_SPEC = pl.BlockSpec(memory_space=pltpu.VMEM)


def cost(macs, nbytes, exps=0):
    return pl.CostEstimate(flops=2 * macs, bytes_accessed=nbytes, transcendentals=exps)


def params():
    return pltpu.CompilerParams(vmem_limit_bytes=VMEM_BYTES)


def member_matrix(channels):
    per_group = channels // GROUPS
    group = lax.broadcasted_iota(jnp.int32, (LANES, channels), 0) * per_group
    channel = lax.broadcasted_iota(jnp.int32, (LANES, channels), 1)
    return jnp.where((channel >= group) & (channel < group + per_group), 1.0, 0.0).astype(F32)


def to_groups(values, member):
    return lax.dot_general(
        values, member, (((1,), (1,)), ((), ())), precision=HIGHEST, preferred_element_type=F32
    )


def to_channels(values, member):
    return jnp.dot(values, member, precision=HIGHEST, preferred_element_type=F32)


def row_label(video_ref, row):
    rows = video_ref.shape[0]
    inside = (row >= 0) & (row < rows)
    return jnp.where(inside, video_ref[jnp.clip(row, 0, rows - 1)], -1)


def row_width(cols_ref, label):
    return jnp.where(label >= 0, cols_ref[jnp.maximum(label, 0)], 0)


def pick(table, label, videos):
    chosen = table[0:1]
    for video in range(1, videos):
        chosen = jnp.where(label == video, table[video : video + 1], chosen)
    return chosen


def norm_tables(stats_ref, gain_ref):
    member = member_matrix(gain_ref.shape[1])
    counts = jnp.maximum(stats_ref[0], 1.0)
    scale = lax.rsqrt(stats_ref[2] / counts + EPSILON)
    return to_channels(stats_ref[1], member), to_channels(scale, member) * gain_ref[...]


def write_stats(out_ref, rows, labels, widths, videos, channels):
    member = member_matrix(channels)
    per_group = channels // GROUPS
    cols = rows[0].shape[0]
    slot = lax.broadcasted_iota(jnp.int32, (SLOTS, 1), 0)
    column = lax.broadcasted_iota(jnp.int32, (cols, 1), 0)
    sums = jnp.zeros((SLOTS, channels), F32)
    counts = jnp.zeros((SLOTS, 1), F32)
    for index, row in enumerate(rows):
        sums = jnp.where(slot == index, jnp.sum(row, axis=0, keepdims=True), sums)
        counts = jnp.where(slot == index, (widths[index] * per_group).astype(F32), counts)
    means = to_groups(sums, member) / jnp.maximum(counts, 1.0)
    means_wide = to_channels(means, member)
    squares = jnp.zeros((SLOTS, channels), F32)
    for index, row in enumerate(rows):
        centered = jnp.where(column < widths[index], row - means_wide[index : index + 1], 0.0)
        squares = jnp.where(
            slot == index, jnp.sum(centered * centered, axis=0, keepdims=True), squares
        )
    spreads = to_groups(squares, member)
    out_ref[...] = jnp.zeros(out_ref.shape, F32)
    for video in range(videos):
        total = jnp.zeros((1, LANES), F32)
        count = jnp.zeros((1, LANES), F32)
        for index in range(len(rows)):
            mine = labels[index] == video
            row_count = counts[index : index + 1]
            total = total + jnp.where(mine, means[index : index + 1] * row_count, 0.0)
            count = count + jnp.where(mine, row_count, 0.0)
        mean = total / jnp.maximum(count, 1.0)
        spread = jnp.zeros((1, LANES), F32)
        for index in range(len(rows)):
            off = means[index : index + 1] - mean
            part = spreads[index : index + 1] + counts[index : index + 1] * off * off
            spread = spread + jnp.where(labels[index] == video, part, 0.0)
        out_ref[0, video : video + 1, :] = count
        out_ref[1, video : video + 1, :] = mean
        out_ref[2, video : video + 1, :] = spread


def place_of(place_ref, video_ref, cols_ref, row_count, rim):
    first = place_ref[0] * row_count
    labels = [row_label(video_ref, first + r) for r in range(-rim, row_count + rim)]
    return labels, [row_width(cols_ref, label) for label in labels]


def build_columns(columns_ref, row_refs):
    padded = columns_ref.shape[0] // len(row_refs)
    for index, row in enumerate(row_refs):
        cells = row().astype(F32)
        count, channels = cells.shape
        cells = jnp.concatenate([cells, jnp.zeros((padded - count, channels), F32)], axis=0)
        start = index * padded
        columns_ref[start : start + padded, 0:channels] = pltpu.roll(cells, 1, 0).astype(BF16)
        columns_ref[start : start + padded, channels : 2 * channels] = cells.astype(BF16)
        columns_ref[start : start + padded, 2 * channels : 3 * channels] = pltpu.roll(
            cells, padded - 1, 0
        ).astype(BF16)


def stats_kernel(place_ref, video_ref, cols_ref, latents_ref, out_ref):
    row_count, cols, channels = latents_ref.shape
    labels, widths = place_of(place_ref, video_ref, cols_ref, row_count, 0)
    column = lax.broadcasted_iota(jnp.int32, (cols, 1), 0)
    rows = [
        jnp.where(column < widths[r], latents_ref[r].astype(F32), 0.0) for r in range(row_count)
    ]
    write_stats(out_ref, rows, labels, widths, cols_ref.shape[0], channels)


def hidden_kernel(
    place_ref, video_ref, cols_ref, before_ref, latents_ref, after_ref, stats_ref, gain_ref,
    shift_ref, out_ref,
):
    row_count, cols, _ = latents_ref.shape
    labels, widths = place_of(place_ref, video_ref, cols_ref, row_count, 1)
    means, scales = norm_tables(stats_ref, gain_ref)
    videos = cols_ref.shape[0]
    column = lax.broadcasted_iota(jnp.int32, (cols, 1), 0)
    for r in range(row_count + 2):
        if r == 0:
            source = before_ref[0]
        elif r == row_count + 1:
            source = after_ref[0]
        else:
            source = latents_ref[r - 1]
        mean = pick(means, labels[r], videos)
        scale = pick(scales, labels[r], videos)
        normed = (source.astype(F32) - mean) * scale + shift_ref[...]
        active = normed / (1.0 + jnp.exp(-normed))
        out_ref[r] = jnp.where(column < widths[r], active, 0.0).astype(BF16)


def conv_kernel(
    last, place_ref, video_ref, cols_ref, hidden_ref, weight_ref, *rest
):
    if last:
        partial_ref, latents_ref, bias_ref, out_ref, stats_ref, columns_ref, total_ref = rest
    else:
        if len(rest) == 4:
            partial_ref, out_ref, columns_ref, total_ref = rest
        else:
            partial_ref = None
            out_ref, columns_ref, total_ref = rest
    tap = pl.program_id(0)
    near_rows = hidden_ref.shape[0]
    row_count = near_rows - 2
    padded = columns_ref.shape[0] // near_rows
    labels, widths = place_of(place_ref, video_ref, cols_ref, row_count, 1)

    @pl.when(tap == 0)
    def _():
        build_columns(
            columns_ref, [functools.partial(hidden_ref.__getitem__, r) for r in range(near_rows)]
        )
        if partial_ref is None:
            total_ref[...] = jnp.zeros(total_ref.shape, F32)
        else:
            total_ref[...] = partial_ref[...]

    start = pl.multiple_of(tap * padded, 16)
    product = jnp.dot(
        columns_ref[pl.ds(start, row_count * padded), :], weight_ref[0], preferred_element_type=F32
    )
    for r in range(row_count):
        lo, hi = r * padded, (r + 1) * padded
        near = jnp.where(tap == 0, labels[r], jnp.where(tap == 1, labels[r + 1], labels[r + 2]))
        total_ref[lo:hi, :] += jnp.where(near == labels[r + 1], product[lo:hi], 0.0)

    @pl.when(tap == 2)
    def _():
        if not last:
            out_ref[...] = total_ref[...]
            return
        cols = latents_ref.shape[1]
        column = lax.broadcasted_iota(jnp.int32, (cols, 1), 0)
        rows = []
        for r in range(row_count):
            branch = total_ref[r * padded : r * padded + cols, :]
            value = latents_ref[r].astype(F32) + branch + bias_ref[...]
            value = jnp.where(column < widths[r + 1], value, 0.0).astype(BF16)
            out_ref[r] = value
            rows.append(value.astype(F32))
        write_stats(
            stats_ref, rows, labels[1:-1], widths[1:-1], cols_ref.shape[0], latents_ref.shape[2]
        )


def normed_pair(pair, labels, means, scales, shift_ref, videos):
    cols = pair.shape[0] // 2
    halves = []
    for half in range(2):
        values = pair[half * cols : (half + 1) * cols]
        mean = pick(means, labels[half], videos)
        scale = pick(scales, labels[half], videos)
        halves.append((values - mean) * scale + shift_ref[...])
    return halves


def query_kernel(
    place_ref, video_ref, cols_ref, own_ref, stats_ref, gain_ref, shift_ref, weight_ref, bias_ref,
    queries_ref, constant_ref,
):
    pairs, double, channels = own_ref.shape
    cols = double // 2
    row_count = 2 * pairs
    labels, widths = place_of(place_ref, video_ref, cols_ref, row_count, 0)
    means, scales = norm_tables(stats_ref, gain_ref)
    videos = cols_ref.shape[0]
    column = lax.broadcasted_iota(jnp.int32, (cols, 1), 0)
    rows = []
    for pair in range(pairs):
        halves = normed_pair(
            own_ref[pair].astype(F32), labels[2 * pair : 2 * pair + 2], means, scales, shift_ref,
            videos,
        )
        for half in range(2):
            rows.append(jnp.where(column < widths[2 * pair + half], halves[half], 0.0))
    cells = jnp.concatenate(rows, axis=0).astype(BF16)
    queries = (
        jnp.dot(cells, weight_ref[:, 0:channels], preferred_element_type=F32)
        + bias_ref[:, 0:channels]
    ).astype(BF16)
    factor = channels ** (-0.5) * math.log2(math.e)
    turned = lax.dot_general(
        queries, weight_ref[:, channels : 2 * channels], (((1,), (1,)), ((), ())),
        preferred_element_type=F32,
    )
    queries_ref[...] = (turned * factor).astype(BF16)
    constant = jnp.sum(
        queries.astype(F32) * bias_ref[:, channels : 2 * channels], axis=1, keepdims=True
    )
    constant_ref[...] = jnp.broadcast_to(constant * factor, constant_ref.shape)


def attend_kernel(
    place_ref, video_ref, cols_ref, own_ref, stats_ref, gain_ref, shift_ref, weight_ref, bias_ref,
    out_weight_ref, out_bias_ref, queries_ref, constant_ref, codes_ref, canvas_ref, out_ref,
    keys_ref, total_ref,
):
    pairs, double, channels = own_ref.shape
    cols = double // 2
    row_count = 2 * pairs
    rows = video_ref.shape[0]
    labels, widths = place_of(place_ref, video_ref, cols_ref, row_count, 0)
    means, scales = norm_tables(stats_ref, gain_ref)
    videos = cols_ref.shape[0]
    lowest, highest = labels[0], labels[-1]

    def count(row, carried):
        below, upto = carried
        label = video_ref[row]
        return (
            below + (label < lowest).astype(jnp.int32),
            upto + (label <= highest).astype(jnp.int32),
        )

    first_row, end_row = lax.fori_loop(0, rows, count, (jnp.int32(0), jnp.int32(0)))
    first_block = (first_row * cols) // KEY_BLOCK
    end_block = (end_row * cols + KEY_BLOCK - 1) // KEY_BLOCK
    first_pair = (first_block * KEY_BLOCK) // double
    end_pair = jnp.minimum((end_block * KEY_BLOCK + double - 1) // double, rows // 2)

    def normalise(pair, carried):
        near = [video_ref[2 * pair], video_ref[2 * pair + 1]]
        halves = normed_pair(
            canvas_ref[pair].astype(F32), near, means, scales, shift_ref, videos
        )
        start = pl.multiple_of(pair * double, 16)
        keys_ref[pl.ds(start, double), :] = jnp.concatenate(halves, axis=0).astype(BF16)
        return carried

    lax.fori_loop(first_pair, end_pair, normalise, jnp.int32(0))

    query_label = jnp.concatenate(
        [jnp.zeros((cols, 1), F32) + labels[r].astype(F32) for r in range(row_count)], axis=0
    )
    queries = queries_ref[...]
    constant = constant_ref[:, 0:1]
    total_ref[...] = jnp.zeros(total_ref.shape, F32)

    def step(block, carried):
        largest, denominator = carried
        start = pl.multiple_of(block * KEY_BLOCK, KEY_BLOCK)
        keys = keys_ref[pl.ds(start, KEY_BLOCK), :]
        scores = lax.dot_general(
            queries, keys, (((1,), (1,)), ((), ())), preferred_element_type=F32
        )
        scores = jnp.where(codes_ref[:, pl.ds(start, KEY_BLOCK)] == query_label, scores, MASKED)
        peak = jnp.maximum(largest, jnp.max(scores, axis=1, keepdims=True) + constant)
        weights = jnp.exp2(scores - (peak - constant))
        factor = jnp.exp2(largest - peak)
        denominator = denominator * factor + jnp.sum(weights, axis=1, keepdims=True)
        total_ref[...] = total_ref[...] * factor + jnp.dot(
            weights.astype(BF16), keys, preferred_element_type=F32
        )
        return peak, denominator

    cells = row_count * cols
    _, denominator = lax.fori_loop(
        first_block, end_block, step,
        (jnp.full((cells, 1), LOWEST, F32), jnp.zeros((cells, 1), F32)),
    )
    mean_cell = (total_ref[...] / denominator).astype(BF16)
    mixed = (
        jnp.dot(mean_cell, weight_ref[:, 2 * channels :], preferred_element_type=F32)
        + bias_ref[:, 2 * channels :]
    ).astype(BF16)
    attended = jnp.dot(mixed, out_weight_ref[...], preferred_element_type=F32) + out_bias_ref[...]
    column = lax.broadcasted_iota(jnp.int32, (cols, 1), 0)
    for pair in range(pairs):
        before = own_ref[pair].astype(F32)
        halves = []
        for half in range(2):
            r = 2 * pair + half
            value = before[half * cols : (half + 1) * cols] + attended[r * cols : (r + 1) * cols]
            halves.append(jnp.where(column < widths[r], value, 0.0))
        out_ref[pair] = jnp.concatenate(halves, axis=0).astype(BF16)


def upsample_kernel(
    place_ref, video_ref, cols_ref, before_ref, own_ref, after_ref, weight_ref, bias_ref, out_ref,
    columns_ref, wide_ref,
):
    row_count, cols, channels = own_ref.shape
    near_rows = row_count + 2
    padded = columns_ref.shape[0] // near_rows
    labels, widths = place_of(place_ref, video_ref, cols_ref, row_count, 1)
    parts_out = wide_ref.shape[0]
    out_channels = out_ref.shape[-1]
    sources = [functools.partial(before_ref.__getitem__, 0)]
    sources += [functools.partial(own_ref.__getitem__, r) for r in range(row_count)]
    sources += [functools.partial(after_ref.__getitem__, 0)]
    build_columns(columns_ref, sources)
    span = row_count * padded
    column = lax.broadcasted_iota(jnp.int32, (2 * cols, 1), 0)
    for down in range(2):
        for right in range(2):
            lanes = slice(right * channels, (right + 2) * channels)
            parts = [
                jnp.dot(
                    columns_ref[(down + tap) * padded : (down + tap) * padded + span, lanes],
                    weight_ref[down, tap, right],
                    preferred_element_type=F32,
                )
                for tap in range(2)
            ]
            rim = parts[down]
            same = parts[1 - down]
            for r in range(row_count):
                lo, hi = r * padded, r * padded + cols
                near = labels[r + 2 * down]
                value = same[lo:hi] + jnp.where(near == labels[r + 1], rim[lo:hi], 0.0)
                for part in range(parts_out):
                    wide_ref[part, 2 * r + down, pl.ds(right, cols, 2), :] = value[
                        :, part * LANES : (part + 1) * LANES
                    ]
    for r in range(2 * row_count):
        valid = column < 2 * widths[r // 2 + 1]
        for part in range(parts_out):
            lo, hi = part * LANES, min((part + 1) * LANES, out_channels)
            value = wide_ref[part, r, :, 0 : hi - lo] + bias_ref[:, lo:hi]
            out_ref[r, :, lo:hi] = jnp.where(valid, value, 0.0).astype(BF16)


def merge_stats(mine, other):
    count = mine[0] + other[0]
    safe = jnp.maximum(count, 1.0)
    off = other[1] - mine[1]
    mean = mine[1] + off * (other[0] / safe)
    spread = mine[2] + other[2] + off * off * (mine[0] * other[0] / safe)
    return jnp.stack([count, mean, spread])


def combined_weight(weight):
    wide = jnp.pad(weight.astype(F32), ((0, 0),) * 3 + ((0, -weight.shape[-1] % LANES),))
    rows = jnp.stack(
        [
            jnp.stack([wide[0], wide[1] + wide[2]]),
            jnp.stack([wide[0] + wide[1], wide[2]]),
        ]
    )
    left = jnp.concatenate([rows[:, :, 0], rows[:, :, 1] + rows[:, :, 2]], axis=2)
    right = jnp.concatenate([rows[:, :, 0] + rows[:, :, 1], rows[:, :, 2]], axis=2)
    return jnp.stack([left, right], axis=2).astype(BF16)


def shards(
    tiles,
    frames,
    latents,
    row_video,
    video_cols,
    first_gain,
    first_shift,
    conv_weight,
    conv_bias,
    second_gain,
    second_shift,
    triple_weight,
    triple_bias,
    output_weight,
    output_bias,
    upsample_weight,
    upsample_bias,
):
    row_count, frame_count, cols, channels = latents.shape
    assert frame_count == 1 and row_count % 2 == 0
    out_channels = upsample_weight.shape[-1]
    rows = row_count * tiles
    cells = row_count * cols
    padded = -(-(cols + 1) // 16) * 16
    near_rows = row_count + 2
    assert (rows * cols) % KEY_BLOCK == 0
    source = latents.reshape(row_count, cols, channels)
    tile = lax.axis_index("tile")
    frame = lax.axis_index("frame")
    place = jnp.reshape(tile, (1,)).astype(jnp.int32)
    turned_place = jnp.reshape(tile // 2 * 2 + frame % 2, (1,)).astype(jnp.int32)

    def number(t, f):
        return t * frames + f

    def turned(t, f):
        return number(t // 2 * 2 + f % 2, f // 2 * 2 + t % 2)

    every = [(t, f) for t in range(tiles) for f in range(frames)]
    turn = [(number(t, f), turned(t, f)) for t, f in every]
    up = [(i, i + 1) for i in range(tiles - 1)]
    down = [(i + 1, i) for i in range(tiles - 1)]

    def row(vector):
        return vector.reshape(1, -1)

    before = lax.ppermute(source[row_count - 1 :], "tile", up)
    after = lax.ppermute(source[:1], "tile", down)
    stats_shape = jax.ShapeDtypeStruct((3, SLOTS, LANES), F32)
    stats = pl.pallas_call(
        stats_kernel,
        out_shape=stats_shape,
        in_specs=[SMEM_SPEC] * 3 + [VMEM_SPEC],
        out_specs=VMEM_SPEC,
        compiler_params=params(),
        cost_estimate=cost(cells * channels * 2, 2 * cells * channels),
        name="first_stats",
    )(place, row_video, video_cols, source)
    bit = 1
    while bit < tiles:
        other = lax.ppermute(stats, "tile", [(i, i ^ bit) for i in range(tiles)])
        stats = merge_stats(stats, other)
        bit *= 2
    hidden = pl.pallas_call(
        hidden_kernel,
        out_shape=jax.ShapeDtypeStruct((near_rows, cols, channels), BF16),
        in_specs=[SMEM_SPEC] * 3 + [VMEM_SPEC] * 6,
        out_specs=VMEM_SPEC,
        compiler_params=params(),
        cost_estimate=cost(cells * channels * 10, 5 * cells * channels, cells * channels),
        name="hidden",
    )(
        place, row_video, video_cols, before, source, after, stats, row(first_gain),
        row(first_shift),
    )

    weights = conv_weight.reshape(9, 3 * channels, channels)
    taps = min(3, frames)
    earlier = [
        lax.ppermute(hidden, "frame", [(i, i + by) for i in range(frames - by)])
        for by in range(1, taps)
    ]
    total = None
    for back, context in enumerate([hidden] + earlier):
        last = back == taps - 1
        time_tap = 2 - back

        def whole(shape):
            return pl.BlockSpec(shape, lambda b, n=len(shape): (0,) * n)

        in_specs = [SMEM_SPEC] * 3 + [
            whole((near_rows, cols, channels)),
            pl.BlockSpec((1, 3 * channels, channels), lambda b, a=time_tap: (3 * a + b, 0, 0)),
        ]
        operands = [place, row_video, video_cols, context, weights]
        if total is not None:
            in_specs.append(whole((row_count * padded, channels)))
            operands.append(total)
        if last:
            in_specs += [whole((row_count, cols, channels)), whole((1, channels))]
            operands += [source, row(conv_bias)]
            out_shape = (jax.ShapeDtypeStruct((row_count, cols, channels), BF16), stats_shape)
            out_specs = (whole((row_count, cols, channels)), whole((3, SLOTS, LANES)))
        else:
            out_shape = jax.ShapeDtypeStruct((row_count * padded, channels), F32)
            out_specs = whole((row_count * padded, channels))
        total = pl.pallas_call(
            functools.partial(conv_kernel, last),
            grid=(3,),
            out_shape=out_shape,
            in_specs=in_specs,
            out_specs=out_specs,
            scratch_shapes=[
                pltpu.VMEM((near_rows * padded, 3 * channels), BF16),
                pltpu.VMEM((row_count * padded, channels), F32),
            ],
            compiler_params=params(),
            cost_estimate=cost(9 * cells * channels * channels, 18 * channels * channels),
            name="conv_last" if last else "conv_part",
        )(*operands)
    after_conv, stats = total

    own = lax.ppermute(after_conv, BOTH, turn)
    stats = lax.ppermute(stats, BOTH, turn)
    groups = [
        [number(t, 2 * j + c) for t in range(side, tiles, 2) for c in range(2)]
        for side in range(2)
        for j in range(frames // 2)
    ]
    canvas = lax.all_gather(own, BOTH, axis=0, tiled=True, axis_index_groups=groups)
    stats = merge_stats(
        stats, lax.ppermute(stats, BOTH, [(number(t, f), number(t, f ^ 1)) for t, f in every])
    )
    bit = 2
    while bit < tiles:
        other = lax.ppermute(
            stats, BOTH, [(number(t, f), number(t ^ bit, f)) for t, f in every]
        )
        stats = merge_stats(stats, other)
        bit *= 2
    own_pairs = own.reshape(row_count // 2, 2 * cols, channels)
    queries, constant = pl.pallas_call(
        query_kernel,
        out_shape=(
            jax.ShapeDtypeStruct((cells, channels), BF16),
            jax.ShapeDtypeStruct((cells, LANES), F32),
        ),
        in_specs=[SMEM_SPEC] * 3 + [VMEM_SPEC] * 6,
        out_specs=(VMEM_SPEC, VMEM_SPEC),
        compiler_params=params(),
        cost_estimate=cost(2 * cells * channels * channels, 4 * cells * channels),
        name="queries",
    )(
        turned_place, row_video, video_cols, own_pairs, stats, row(second_gain),
        row(second_shift), triple_weight, row(triple_bias),
    )
    widths = jnp.sum(
        jnp.where(
            row_video[:, None] == jnp.arange(video_cols.shape[0], dtype=jnp.int32)[None, :],
            video_cols[None, :],
            0,
        ),
        axis=1,
    )
    valid = jnp.arange(cols, dtype=jnp.int32)[None, :] < widths[:, None]
    codes = jnp.where(valid, row_video[:, None], -1).astype(F32).reshape(1, rows * cols)
    attended = pl.pallas_call(
        attend_kernel,
        out_shape=jax.ShapeDtypeStruct((row_count // 2, 2 * cols, channels), BF16),
        in_specs=[SMEM_SPEC] * 3 + [VMEM_SPEC] * 12,
        out_specs=VMEM_SPEC,
        scratch_shapes=[
            pltpu.VMEM((rows * cols, channels), BF16),
            pltpu.VMEM((cells, channels), F32),
        ],
        compiler_params=params(),
        cost_estimate=cost(
            2 * cells * rows * cols * channels, 2 * rows * cols * channels, cells * rows * cols
        ),
        name="attend",
    )(
        turned_place, row_video, video_cols, own_pairs, stats, row(second_gain),
        row(second_shift), triple_weight, row(triple_bias), output_weight, row(output_bias),
        queries, constant, codes, canvas.reshape(rows // 2, 2 * cols, channels),
    )
    attended = attended.reshape(row_count, cols, channels)

    places = {turned(t, f): (t, f) for t, f in every}
    assert all(places[turned(t, f)] == (t, f) for t, f in every)
    back_up = [(turned(t, f), number(t + 1, f)) for t, f in every if t + 1 < tiles]
    back_down = [(turned(t, f), number(t - 1, f)) for t, f in every if t > 0]
    before = lax.ppermute(attended[row_count - 1 :], BOTH, back_up)
    after = lax.ppermute(attended[:1], BOTH, back_down)
    home = lax.ppermute(attended, BOTH, turn)
    decoded = pl.pallas_call(
        upsample_kernel,
        out_shape=jax.ShapeDtypeStruct((2 * row_count, 2 * cols, out_channels), BF16),
        in_specs=[SMEM_SPEC] * 3 + [VMEM_SPEC] * 5,
        out_specs=VMEM_SPEC,
        scratch_shapes=[
            pltpu.VMEM((near_rows * padded, 3 * channels), BF16),
            pltpu.VMEM((-(-out_channels // LANES), 2 * row_count, 2 * cols, LANES), F32),
        ],
        compiler_params=params(),
        cost_estimate=cost(16 * cells * channels * out_channels, 8 * cells * out_channels),
        name="upsample",
    )(
        place, row_video, video_cols, before, home, after, combined_weight(upsample_weight),
        row(upsample_bias),
    )
    return decoded.reshape(2 * row_count, 1, 2 * cols, out_channels)


def solution(mesh):
    sizes = dict(mesh.shape)
    in_specs = (P("tile", "frame", None, None),) + (P(),) * 14
    out_specs = P("tile", "frame", None, None)
    body = functools.partial(shards, sizes["tile"], sizes["frame"])
    return jax.shard_map(body, mesh=mesh, in_specs=in_specs, out_specs=out_specs, check_vma=False)
```

time: 404 us -> 155 us (0.38)
  the two profiles are of different devices: /device:TPU:8 before, /device:TPU:17 now
where the time goes in v1:
time: 155 us
  waiting for transfers between devices  59.6 us (38%)
  starting transfers between devices  38.6 us (25%)
  Pallas kernels  25.3 us (16%)
  between operations  13.9 us (9%)
  local copies, waits for them, and re-layouts  12.5 us (8%)
  other arithmetic  5.05 us (3%)
    all_gather x1, waiting for transfers between devices, shards(): lax.all_gather(own, BOTH, axis=0, tiled=True, axis_index_groups=groups)  35.4 us
    pallas_call x1, Pallas kernels, shards(): pl.pallas_call(attend_kernel, out_shape=jax.ShapeDtypeStruct((row_count /...  10.8 us
    ppermute x1, starting transfers between devices, shards(): home = lax.ppermute(attended, BOTH, turn)  10.6 us
    unnamed x45, local copies, waits for them, and re-layouts  9.7 us
    pallas_call x2, Pallas kernels, shards(): pl.pallas_call(functools.partial(conv_kernel, last), grid=(3,), out_shape...  7.61 us
    ppermute x1, starting transfers between devices, shards(): after = lax.ppermute(source[:1], 'tile', down)  6.25 us
    ppermute x3, waiting for transfers between devices, shards(): lax.ppermute(stats, BOTH, [(number(t, f), number(t ^ bit, f)) for t, f in...  5.99 us
    ppermute x1, starting transfers between devices, shards(): own = lax.ppermute(after_conv, BOTH, turn)  4.98 us
  transfers between devices with their start and end apart: 17, of which 14 were waited for; matrix products, arithmetic and copies ran while one was open for 5% of the time, Pallas kernels for 3%

profile of v1, /device:TPU:17, one launch (start us, length us, event | category | flops | bytes accessed | tf_op | source)
XLA Modules:
  0.0 154.9 jit_solution(3996715864041653987)
XLA Ops:
  8.8 1.8 %first_stats.1 = f32[3,8,128]{2,1,0:T(8,128)S(1)} custom-call(s32[1]{0:T(128)} %bitcast.place_ref, s32[64]{0:T(128)S(1)} %copy-done.7, s32[2]{0:T(128)S(1)} %copy-done.9, bf16[4,104,384]{2,1,0:T(8,128)(2,1)S(1)} %bitcast.35), custom_call_target="tpu_custom_call" | custom-call | flops 638976 | bytes 319488 | tf_op jit(solution)/shard_map/first_stats/pallas_call | solution.py:474
  16.0 1.4 collective-permute-start.4
  18.7 6.3 %collective-permute-start.1 = (bf16[1,104,384]{2,1,0:T(8,128)(2,1)S(1)}, bf16[1,104,384]{2,1,0:T(8,128)(2,1)S(1)}, u32[]{:S(2)}, u32[]{:S(2)}) collective-permute-start(bf16[1,104,384]{2,1,0:T(8,128)(2,1)S(1)} %get-tuple-element.39), channel_id=1, source_target_pairs={{2,0},{4,2},{6,4},{8,6},{10,8},{12,10},{14,12},{16,14},{18,16},{20... | collective-permute-start | bytes 239624 | tf_op jit(solution)/shard_map/ppermute | solution.py:472
  25.0 1.9 %collective-permute-start = (bf16[1,104,384]{2,1,0:T(8,128)(2,1)S(1)}, bf16[1,104,384]{2,1,0:T(8,128)(2,1)S(1)}, u32[]{:S(2)}, u32[]{:S(2)}) collective-permute-start(bf16[1,104,384]{2,1,0:T(8,128)(2,1)S(1)} %get-tuple-element.40), channel_id=1, source_target_pairs={{0,2},{2,4},{4,6},{6,8},{8,10},{10,12},{12,14},{14,16},{16,18},{18... | collective-permute-start | bytes 239624 | tf_op jit(solution)/shard_map/ppermute | solution.py:471
  28.3 3.6 %collective-permute-done.before_ref = bf16[1,104,384]{2,1,0:T(8,128)(2,1)S(1)} collective-permute-done((bf16[1,104,384]{2,1,0:T(8,128)(2,1)S(1)}, bf16[1,104,384]{2,1,0:T(8,128)(2,1)S(1)}, u32[]{:S(2)}, u32[]{:S(2)}) %collective-permute-start) | collective-permute-done | bytes 79904 | tf_op jit(solution)/shard_map/ppermute | solution.py:471
  34.6 3.3 %copy-done = bf16[3,3,3,384,384]{4,3,2,1,0:T(8,128)(2,1)S(1)} copy-done((bf16[3,3,3,384,384]{4,3,2,1,0:T(8,128)(2,1)S(1)}, bf16[3,3,3,384,384]{4,3,2,1,0:T(8,128)(2,1)}, u32[]{:S(2)}) %copy-start) | copy-done | bytes 7962648
  37.8 3.2 %conv_part.1.rest_0_ = f32[448,384]{1,0:T(8,128)S(1)} custom-call(s32[1]{0:T(128)} %bitcast.place_ref, s32[64]{0:T(128)S(1)} %copy-done.7, s32[2]{0:T(128)S(1)} %copy-done.9, bf16[6,104,384]{2,1,0:T(8,128)(2,1)S(1)} %hidden.1.hidden_ref, bf16[9,1152,384]{2,1,0:T(8,128)(2,1)S(1)} %bitcast.33), custom_call_target="tpu_custom_call" | custom-call | flops 1104150528 | bytes 2654208 | tf_op jit(solution)/shard_map/conv_part/pallas_call | solution.py:531
  41.7 4.5 %conv_last.1 = (bf16[4,104,384]{2,1,0:T(8,128)(2,1)S(1)}, f32[3,8,128]{2,1,0:T(8,128)S(1)}) custom-call(s32[1]{0:T(128)} %bitcast.place_ref, s32[64]{0:T(128)S(1)} %copy-done.7, s32[2]{0:T(128)S(1)} %copy-done.9, bf16[6,104,384]{2,1,0:T(8,128)(2,1)S(1)} %collective-permute-done.6.hidden_ref, bf16[9,1152,384]{2,1,0:T(8,128)(2,1)S(1)} %bitcast.34, ...), custom_call_target="tpu_custom_call" | custom-call | flops 1104150528 | bytes 2654208 | tf_op jit(solution)/shard_map/conv_last/pallas_call | solution.py:531
  46.2 5.0 %collective-permute-start.7 = (bf16[4,104,384]{2,1,0:T(8,128)(2,1)S(1)}, bf16[4,104,384]{2,1,0:T(8,128)(2,1)S(1)}, u32[]{:S(2)}, u32[]{:S(2)}) collective-permute-start(bf16[4,104,384]{2,1,0:T(8,128)(2,1)S(1)} %get-tuple-element.9), channel_id=1, source_target_pairs={{0,0},{1,2},{2,1},{3,3},{4,4},{5,6},{6,5},{7,7},{8,8},{9,10},{10,9... | collective-permute-start | bytes 958472 | tf_op jit(solution)/shard_map/ppermute | solution.py:547
  51.1 4.7 %collective-permute-done.7 = bf16[4,104,384]{2,1,0:T(8,128)(2,1)S(1)} collective-permute-done((bf16[4,104,384]{2,1,0:T(8,128)(2,1)S(1)}, bf16[4,104,384]{2,1,0:T(8,128)(2,1)S(1)}, u32[]{:S(2)}, u32[]{:S(2)}) %collective-permute-start.7) | collective-permute-done | bytes 319520 | tf_op jit(solution)/shard_map/ppermute | solution.py:547
  58.7 3.6 %collective-permute-start.8 = (f32[3,8,128]{2,1,0:T(8,128)S(1)}, f32[3,8,128]{2,1,0:T(8,128)S(1)}, u32[]{:S(2)}, u32[]{:S(2)}) collective-permute-start(f32[3,8,128]{2,1,0:T(8,128)S(1)} %get-tuple-element.10), channel_id=1, source_target_pairs={{0,0},{1,2},{2,1},{3,3},{4,4},{5,6},{6,5},{7,7},{8,8},{9,10},{10,9... | collective-permute-start | bytes 36872 | tf_op jit(solution)/shard_map/ppermute | solution.py:548
  65.3 2.8 %collective-permute-done.10 = f32[3,8,128]{2,1,0:T(8,128)S(1)} collective-permute-done((f32[3,8,128]{2,1,0:T(8,128)S(1)}, f32[3,8,128]{2,1,0:T(8,128)S(1)}, u32[]{:S(2)}, u32[]{:S(2)}) %collective-permute-start.10) | collective-permute-done | bytes 12320 | tf_op jit(solution)/shard_map/ppermute | solution.py:560
  68.2 1.3 maximum_bitcast_fusion.2
  69.5 1.7 %collective-permute-done.11 = f32[3,8,128]{2,1,0:T(8,128)S(1)} collective-permute-done((f32[3,8,128]{2,1,0:T(8,128)S(1)}, f32[3,8,128]{2,1,0:T(8,128)S(1)}, u32[]{:S(2)}, u32[]{:S(2)}) %collective-permute-start.11) | collective-permute-done | bytes 12320 | tf_op jit(solution)/shard_map/ppermute | solution.py:560
  73.2 1.5 collective-permute-done.12
  74.8 1.5 queries.1
  76.3 35.4 %all-gather.2.cloned.1.call-done = bf16[64,104,384]{2,1,0:T(8,128)(2,1)} async-done(((bf16[4,104,384]{2,1,0:T(8,128)(2,1)}), bf16[64,104,384]{2,1,0:T(8,128)(2,1)}) %all-gather.2.cloned.1.call-update) | async-done | bytes 5111824 | tf_op jit(solution)/shard_map/all_gather | solution.py:554
  111.8 2.4 %copy-done.12 = bf16[64,104,384]{2,1,0:T(8,128)(2,1)S(1)} copy-done((bf16[64,104,384]{2,1,0:T(8,128)(2,1)S(1)}, bf16[64,104,384]{2,1,0:T(8,128)(2,1)}, u32[]{:S(2)}) %copy-start.12) | copy-done | bytes 5111832
  114.2 10.8 %attend.1 = bf16[2,208,384]{2,1,0:T(8,128)(2,1)S(1)} custom-call(s32[1]{0:T(128)} %bitcast.1.place_ref, s32[64]{0:T(128)S(1)} %copy-done.8, s32[2]{0:T(128)S(1)} %copy-done.10, bf16[2,208,384]{2,1,0:T(8,128)(2,1)S(1)} %bitcast.40, f32[3,8,128]{2,1,0:T(8,128)S(1)} %pad_maximum_fusion.9.stats_ref, f32[1,384]{1,0:T(1,128)S(1)} %reshape.105.gain_ref, ...), custom_call_target="tpu_custom_call" | custom-call | flops 4253024256 | bytes 5111808 | tf_op jit(solution)/shard_map/attend/pallas_call | solution.py:591
  125.0 10.6 %collective-permute-start.14 = (bf16[4,104,384]{2,1,0:T(8,128)(2,1)S(1)}, bf16[4,104,384]{2,1,0:T(8,128)(2,1)S(1)}, u32[]{:S(2)}, u32[]{:S(2)}) collective-permute-start(bf16[4,104,384]{2,1,0:T(8,128)(2,1)S(1)} %bitcast.41), channel_id=1, source_target_pairs={{0,0},{1,2},{2,1},{3,3},{4,4},{5,6},{6,5},{7,7},{8,8},{9,10},{10,9... | collective-permute-start | bytes 958472 | tf_op jit(solution)/shard_map/ppermute | solution.py:618
  135.6 1.9 %collective-permute-start.15 = (bf16[1,104,384]{2,1,0:T(8,128)(2,1)S(1)}, bf16[1,104,384]{2,1,0:T(8,128)(2,1)S(1)}, u32[]{:S(2)}, u32[]{:S(2)}) collective-permute-start(bf16[1,104,384]{2,1,0:T(8,128)(2,1)S(1)} %get-tuple-element.37), channel_id=1, source_target_pairs={{1,0},{3,1},{4,2},{6,3},{5,4},{7,5},{8,6},{10,7},{9,8},{11,9},{12,... | collective-permute-start | bytes 239624 | tf_op jit(solution)/shard_map/ppermute | solution.py:617
  137.5 3.4 %collective-permute-start.13 = (bf16[1,104,384]{2,1,0:T(8,128)(2,1)S(1)}, bf16[1,104,384]{2,1,0:T(8,128)(2,1)S(1)}, u32[]{:S(2)}, u32[]{:S(2)}) collective-permute-start(bf16[1,104,384]{2,1,0:T(8,128)(2,1)S(1)} %get-tuple-element.38), channel_id=1, source_target_pairs={{0,2},{2,3},{1,4},{3,5},{4,6},{6,7},{5,8},{7,9},{8,10},{10,11},{9,... | collective-permute-start | bytes 239624 | tf_op jit(solution)/shard_map/ppermute | solution.py:616
  141.4 3.1 %collective-permute-done.13.before_ref = bf16[1,104,384]{2,1,0:T(8,128)(2,1)S(1)} collective-permute-done((bf16[1,104,384]{2,1,0:T(8,128)(2,1)S(1)}, bf16[1,104,384]{2,1,0:T(8,128)(2,1)S(1)}, u32[]{:S(2)}, u32[]{:S(2)}) %collective-permute-start.13) | collective-permute-done | bytes 79904 | tf_op jit(solution)/shard_map/ppermute | solution.py:616
  144.5 2.3 %upsample.1 = bf16[8,208,192]{2,1,0:T(8,128)(2,1)S(1)} custom-call(s32[1]{0:T(128)} %bitcast.place_ref, s32[64]{0:T(128)S(1)} %copy-done.8, s32[2]{0:T(128)S(1)} %copy-done.10, bf16[1,104,384]{2,1,0:T(8,128)(2,1)S(1)} %collective-permute-done.13.before_ref, bf16[4,104,384]{2,1,0:T(8,128)(2,1)S(1)} %collective-permute-done.14.own_ref, ...), custom_call_target="tpu_custom_call" | custom-call | flops 981467136 | bytes 638976 | tf_op jit(solution)/shard_map/upsample/pallas_call | solution.py:619
  (108 shorter events, 23.1 us)
Async XLA Ops:
  6.5 28.0 %copy-start.18 = (f32[384]{0:T(512)S(1)}, f32[384]{0:T(512)}, u32[]{:S(2)}) copy-start(f32[384]{0:T(512)} %param.21) | copy-start | bytes 4612
  6.5 105.2 %all-gather.2.cloned.1.call-start = ((), (), s32[]{:S(2)}) async-start(), calls=%async_computation | async-start | bytes 5431296 | tf_op jit(solution)/shard_map/all_gather | solution.py:554
  10.7 2.6 %collective-permute-start.2 = (f32[3,8,128]{2,1,0:T(8,128)S(1)}, f32[3,8,128]{2,1,0:T(8,128)S(1)}, u32[]{:S(2)}, u32[]{:S(2)}) collective-permute-start(f32[3,8,128]{2,1,0:T(8,128)S(1)} %first_stats.1), channel_id=1, source_target_pairs={{0,2},{2,0},{4,6},{6,4},{8,10},{10,8},{12,14},{14,12},{16,18},{18,... | collective-permute-start | bytes 36872 | tf_op jit(solution)/shard_map/ppermute | solution.py:485
  13.3 2.6 %collective-permute-start.3 = (f32[3,8,128]{2,1,0:T(8,128)S(1)}, f32[3,8,128]{2,1,0:T(8,128)S(1)}, u32[]{:S(2)}, u32[]{:S(2)}) collective-permute-start(f32[3,8,128]{2,1,0:T(8,128)S(1)} %pad_maximum_fusion.2), channel_id=1, source_target_pairs={{0,4},{2,6},{4,0},{6,2},{8,12},{10,14},{12,8},{14,10},{16,20},{18,... | collective-permute-start | bytes 36872 | tf_op jit(solution)/shard_map/ppermute | solution.py:485
  16.0 2.6 %collective-permute-start.4 = (f32[3,8,128]{2,1,0:T(8,128)S(1)}, f32[3,8,128]{2,1,0:T(8,128)S(1)}, u32[]{:S(2)}, u32[]{:S(2)}) collective-permute-start(f32[3,8,128]{2,1,0:T(8,128)S(1)} %pad_maximum_fusion.3), channel_id=1, source_target_pairs={{0,8},{2,10},{4,12},{6,14},{8,0},{10,2},{12,4},{14,6},{16,24},{18,... | collective-permute-start | bytes 36872 | tf_op jit(solution)/shard_map/ppermute | solution.py:485
  18.6 9.7 %collective-permute-start.5 = (f32[3,8,128]{2,1,0:T(8,128)S(1)}, f32[3,8,128]{2,1,0:T(8,128)S(1)}, u32[]{:S(2)}, u32[]{:S(2)}) collective-permute-start(f32[3,8,128]{2,1,0:T(8,128)S(1)} %pad_maximum_fusion.4), channel_id=1, source_target_pairs={{0,16},{2,18},{4,20},{6,22},{8,24},{10,26},{12,28},{14,30},{16,0},... | collective-permute-start | bytes 36872 | tf_op jit(solution)/shard_map/ppermute | solution.py:485
  18.7 9.6 %collective-permute-start.1 = (bf16[1,104,384]{2,1,0:T(8,128)(2,1)S(1)}, bf16[1,104,384]{2,1,0:T(8,128)(2,1)S(1)}, u32[]{:S(2)}, u32[]{:S(2)}) collective-permute-start(bf16[1,104,384]{2,1,0:T(8,128)(2,1)S(1)} %get-tuple-element.39), channel_id=1, source_target_pairs={{2,0},{4,2},{6,4},{8,6},{10,8},{12,10},{14,12},{16,14},{18,16},{20... | collective-permute-start | bytes 239624 | tf_op jit(solution)/shard_map/ppermute | solution.py:472
  25.0 7.0 %collective-permute-start = (bf16[1,104,384]{2,1,0:T(8,128)(2,1)S(1)}, bf16[1,104,384]{2,1,0:T(8,128)(2,1)S(1)}, u32[]{:S(2)}, u32[]{:S(2)}) collective-permute-start(bf16[1,104,384]{2,1,0:T(8,128)(2,1)S(1)} %get-tuple-element.40), channel_id=1, source_target_pairs={{0,2},{2,4},{4,6},{6,8},{8,10},{10,12},{12,14},{14,16},{16,18},{18... | collective-permute-start | bytes 239624 | tf_op jit(solution)/shard_map/ppermute | solution.py:471
  33.2 8.4 %collective-permute-start.6 = (bf16[6,104,384]{2,1,0:T(8,128)(2,1)S(1)}, bf16[6,104,384]{2,1,0:T(8,128)(2,1)S(1)}, u32[]{:S(2)}, u32[]{:S(2)}) collective-permute-start(bf16[6,104,384]{2,1,0:T(8,128)(2,1)S(1)} %hidden.1.hidden_ref), channel_id=1, source_target_pairs={{0,1},{2,3},{4,5},{6,7},{8,9},{10,11},{12,13},{14,15},{16,17},{18,... | collective-permute-start | bytes 1437704 | tf_op jit(solution)/shard_map/ppermute | solution.py:504
  37.8 3.9 %copy-start.3 = (bf16[4,1,104,384]{3,2,1,0:T(8,128)(2,1)S(1)}, bf16[4,1,104,384]{3,2,1,0:T(8,128)(2,1)}, u32[]{:S(2)}) copy-start(bf16[4,1,104,384]{3,2,1,0:T(8,128)(2,1)} %param.15) | copy-start | bytes 958468
  41.0 15.6 %copy-start.16 = (bf16[3,3,384,192]{2,3,1,0:T(8,128)(2,1)S(1)}, bf16[3,3,384,192]{2,3,1,0:T(8,128)(2,1)}, u32[]{:S(2)}) copy-start(bf16[3,3,384,192]{2,3,1,0:T(8,128)(2,1)} %param.28) | copy-start | bytes 3981316
  46.2 9.6 %collective-permute-start.7 = (bf16[4,104,384]{2,1,0:T(8,128)(2,1)S(1)}, bf16[4,104,384]{2,1,0:T(8,128)(2,1)S(1)}, u32[]{:S(2)}, u32[]{:S(2)}) collective-permute-start(bf16[4,104,384]{2,1,0:T(8,128)(2,1)S(1)} %get-tuple-element.9), channel_id=1, source_target_pairs={{0,0},{1,2},{2,1},{3,3},{4,4},{5,6},{6,5},{7,7},{8,8},{9,10},{10,9... | collective-permute-start | bytes 958472 | tf_op jit(solution)/shard_map/ppermute | solution.py:547
  58.7 5.0 %collective-permute-start.8 = (f32[3,8,128]{2,1,0:T(8,128)S(1)}, f32[3,8,128]{2,1,0:T(8,128)S(1)}, u32[]{:S(2)}, u32[]{:S(2)}) collective-permute-start(f32[3,8,128]{2,1,0:T(8,128)S(1)} %get-tuple-element.10), channel_id=1, source_target_pairs={{0,0},{1,2},{2,1},{3,3},{4,4},{5,6},{6,5},{7,7},{8,8},{9,10},{10,9... | collective-permute-start | bytes 36872 | tf_op jit(solution)/shard_map/ppermute | solution.py:548
  63.8 1.2 collective-permute-start.9
  65.0 3.1 %collective-permute-start.10 = (f32[3,8,128]{2,1,0:T(8,128)S(1)}, f32[3,8,128]{2,1,0:T(8,128)S(1)}, u32[]{:S(2)}, u32[]{:S(2)}) collective-permute-start(f32[3,8,128]{2,1,0:T(8,128)S(1)} %pad_maximum_fusion.6), channel_id=1, source_target_pairs={{0,4},{1,5},{2,6},{3,7},{4,0},{5,1},{6,2},{7,3},{8,12},{9,13},{10,... | collective-permute-start | bytes 36872 | tf_op jit(solution)/shard_map/ppermute | solution.py:560
  68.1 3.1 %collective-permute-start.11 = (f32[3,8,128]{2,1,0:T(8,128)S(1)}, f32[3,8,128]{2,1,0:T(8,128)S(1)}, u32[]{:S(2)}, u32[]{:S(2)}) collective-permute-start(f32[3,8,128]{2,1,0:T(8,128)S(1)} %pad_maximum_fusion.7), channel_id=1, source_target_pairs={{0,8},{1,9},{2,10},{3,11},{4,12},{5,13},{6,14},{7,15},{8,0},{9,1},... | collective-permute-start | bytes 36872 | tf_op jit(solution)/shard_map/ppermute | solution.py:560
  71.2 3.5 %collective-permute-start.12 = (f32[3,8,128]{2,1,0:T(8,128)S(1)}, f32[3,8,128]{2,1,0:T(8,128)S(1)}, u32[]{:S(2)}, u32[]{:S(2)}) collective-permute-start(f32[3,8,128]{2,1,0:T(8,128)S(1)} %pad_maximum_fusion.8), channel_id=1, source_target_pairs={{0,16},{1,17},{2,18},{3,19},{4,20},{5,21},{6,22},{7,23},{8,24},{9,... | collective-permute-start | bytes 36872 | tf_op jit(solution)/shard_map/ppermute | solution.py:560
  71.7 40.0 %copy-start.13 = (bf16[384,384]{1,0:T(8,128)(2,1)S(1)}, bf16[384,384]{1,0:T(8,128)(2,1)}, u32[]{:S(2)}) copy-start(bf16[384,384]{1,0:T(8,128)(2,1)} %out_weight_ref.1) | copy-start | bytes 884740
  114.2 26.7 %copy-start.14 = (bf16[2,2,1,768,256]{4,3,2,1,0:T(8,128)(2,1)S(1)}, bf16[2,2,1,768,256]{4,3,2,1,0:T(8,128)(2,1)}, u32[]{:S(2)}) copy-start(bf16[2,2,1,768,256]{4,3,2,1,0:T(8,128)(2,1)} %maximum_bitcast_fusion.2) | copy-start | bytes 4718596
  114.2 26.7 %copy-start.15 = (bf16[2,2,1,768,256]{4,3,2,1,0:T(8,128)(2,1)S(1)}, bf16[2,2,1,768,256]{4,3,2,1,0:T(8,128)(2,1)}, u32[]{:S(2)}) copy-start(bf16[2,2,1,768,256]{4,3,2,1,0:T(8,128)(2,1)} %maximum_bitcast_fusion.3) | copy-start | bytes 4718596
  125.0 19.5 %collective-permute-start.14 = (bf16[4,104,384]{2,1,0:T(8,128)(2,1)S(1)}, bf16[4,104,384]{2,1,0:T(8,128)(2,1)S(1)}, u32[]{:S(2)}, u32[]{:S(2)}) collective-permute-start(bf16[4,104,384]{2,1,0:T(8,128)(2,1)S(1)} %bitcast.41), channel_id=1, source_target_pairs={{0,0},{1,2},{2,1},{3,3},{4,4},{5,6},{6,5},{7,7},{8,8},{9,10},{10,9... | collective-permute-start | bytes 958472 | tf_op jit(solution)/shard_map/ppermute | solution.py:618
  135.6 5.8 %collective-permute-start.15 = (bf16[1,104,384]{2,1,0:T(8,128)(2,1)S(1)}, bf16[1,104,384]{2,1,0:T(8,128)(2,1)S(1)}, u32[]{:S(2)}, u32[]{:S(2)}) collective-permute-start(bf16[1,104,384]{2,1,0:T(8,128)(2,1)S(1)} %get-tuple-element.37), channel_id=1, source_target_pairs={{1,0},{3,1},{4,2},{6,3},{5,4},{7,5},{8,6},{10,7},{9,8},{11,9},{12,... | collective-permute-start | bytes 239624 | tf_op jit(solution)/shard_map/ppermute | solution.py:617
  137.5 7.0 %copy-start.11 = (f32[192]{0:T(256)S(1)}, f32[192]{0:T(256)}, u32[]{:S(2)}) copy-start(f32[192]{0:T(256)} %param.29) | copy-start | bytes 2308
  137.5 7.0 %collective-permute-start.13 = (bf16[1,104,384]{2,1,0:T(8,128)(2,1)S(1)}, bf16[1,104,384]{2,1,0:T(8,128)(2,1)S(1)}, u32[]{:S(2)}, u32[]{:S(2)}) collective-permute-start(bf16[1,104,384]{2,1,0:T(8,128)(2,1)S(1)} %get-tuple-element.38), channel_id=1, source_target_pairs={{0,2},{2,3},{1,4},{3,5},{4,6},{6,7},{5,8},{7,9},{8,10},{10,11},{9,... | collective-permute-start | bytes 239624 | tf_op jit(solution)/shard_map/ppermute | solution.py:616
  (15 other events, 26.0 us)
Sparse Core Ops, SparseCore 0:
  56.7 55.0 all-gather.1

commit v2 on v1

v2 whole, which is shorter than its diff:
```python
import functools
import math

import jax
import jax.numpy as jnp
from jax import lax
from jax.experimental import pallas as pl
from jax.experimental.pallas import tpu as pltpu
from jax.sharding import PartitionSpec as P

GROUPS = 32
EPSILON = 1e-05
MASKED = -1e30
LOWEST = -5e29
HIGHEST = lax.Precision.HIGHEST
SLOTS = 8
LANES = 128
CHUNKS = 2
VMEM_BYTES = 40 * 1024 * 1024
CONV_VMEM_BYTES = 56 * 1024 * 1024
F32 = jnp.float32
BF16 = jnp.bfloat16

SMEM_SPEC = pl.BlockSpec(memory_space=pltpu.SMEM)
VMEM_SPEC = pl.BlockSpec(memory_space=pltpu.VMEM)


def cost(macs, nbytes, exps=0):
    return pl.CostEstimate(flops=2 * macs, bytes_accessed=nbytes, transcendentals=exps)


def params():
    return pltpu.CompilerParams(vmem_limit_bytes=VMEM_BYTES)


def member_matrix(channels):
    per_group = channels // GROUPS
    group = lax.broadcasted_iota(jnp.int32, (LANES, channels), 0) * per_group
    channel = lax.broadcasted_iota(jnp.int32, (LANES, channels), 1)
    return jnp.where((channel >= group) & (channel < group + per_group), 1.0, 0.0).astype(F32)


def to_groups(values, member):
    return lax.dot_general(
        values, member, (((1,), (1,)), ((), ())), precision=HIGHEST, preferred_element_type=F32
    )


def to_channels(values, member):
    return jnp.dot(values, member, precision=HIGHEST, preferred_element_type=F32)


class Info:
    def __init__(self, ref, rows):
        self.ref, self.rows = ref, rows
        self.videos = ref.shape[0] - 1 - rows

    def tile(self):
        return self.ref[0]

    def label(self, row):
        inside = (row >= 0) & (row < self.rows)
        return jnp.where(inside, self.ref[1 + jnp.clip(row, 0, self.rows - 1)], -1)

    def width(self, label):
        return jnp.where(label >= 0, self.ref[1 + self.rows + jnp.maximum(label, 0)], 0)

    def window(self, first, count):
        labels = [self.label(first + r) for r in range(count)]
        return labels, [self.width(label) for label in labels]


def pick(table, label, videos):
    chosen = table[0:1]
    for video in range(1, videos):
        chosen = jnp.where(label == video, table[video : video + 1], chosen)
    return chosen


def norm_tables(stats_ref, gain_ref):
    member = member_matrix(gain_ref.shape[1])
    counts = jnp.maximum(stats_ref[0], 1.0)
    scale = lax.rsqrt(stats_ref[2] / counts + EPSILON)
    return to_channels(stats_ref[1], member), to_channels(scale, member) * gain_ref[...]


def write_stats(out_ref, rows, labels, widths, videos, channels):
    member = member_matrix(channels)
    per_group = channels // GROUPS
    cols = rows[0].shape[0]
    slot = lax.broadcasted_iota(jnp.int32, (SLOTS, 1), 0)
    column = lax.broadcasted_iota(jnp.int32, (cols, 1), 0)
    sums = jnp.zeros((SLOTS, channels), F32)
    counts = jnp.zeros((SLOTS, 1), F32)
    for index, row in enumerate(rows):
        sums = jnp.where(slot == index, jnp.sum(row, axis=0, keepdims=True), sums)
        counts = jnp.where(slot == index, (widths[index] * per_group).astype(F32), counts)
    means = to_groups(sums, member) / jnp.maximum(counts, 1.0)
    means_wide = to_channels(means, member)
    squares = jnp.zeros((SLOTS, channels), F32)
    for index, row in enumerate(rows):
        centered = jnp.where(column < widths[index], row - means_wide[index : index + 1], 0.0)
        squares = jnp.where(
            slot == index, jnp.sum(centered * centered, axis=0, keepdims=True), squares
        )
    spreads = to_groups(squares, member)
    out_ref[...] = jnp.zeros(out_ref.shape, F32)
    for video in range(videos):
        total = jnp.zeros((1, LANES), F32)
        count = jnp.zeros((1, LANES), F32)
        for index in range(len(rows)):
            mine = labels[index] == video
            row_count = counts[index : index + 1]
            total = total + jnp.where(mine, means[index : index + 1] * row_count, 0.0)
            count = count + jnp.where(mine, row_count, 0.0)
        mean = total / jnp.maximum(count, 1.0)
        spread = jnp.zeros((1, LANES), F32)
        for index in range(len(rows)):
            off = means[index : index + 1] - mean
            part = spreads[index : index + 1] + counts[index : index + 1] * off * off
            spread = spread + jnp.where(labels[index] == video, part, 0.0)
        out_ref[0, video : video + 1, :] = count
        out_ref[1, video : video + 1, :] = mean
        out_ref[2, video : video + 1, :] = spread


def build_columns(columns_ref, row_refs):
    padded = columns_ref.shape[0] // len(row_refs)
    for index, row in enumerate(row_refs):
        cells = row().astype(F32)
        count, channels = cells.shape
        cells = jnp.concatenate([cells, jnp.zeros((padded - count, channels), F32)], axis=0)
        start = index * padded
        columns_ref[start : start + padded, 0:channels] = pltpu.roll(cells, 1, 0).astype(BF16)
        columns_ref[start : start + padded, channels : 2 * channels] = cells.astype(BF16)
        columns_ref[start : start + padded, 2 * channels : 3 * channels] = pltpu.roll(
            cells, padded - 1, 0
        ).astype(BF16)


def stats_kernel(rows, info_ref, latents_ref, out_ref):
    info = Info(info_ref, rows)
    row_count, cols, channels = latents_ref.shape
    labels, widths = info.window(info.tile() * row_count, row_count)
    column = lax.broadcasted_iota(jnp.int32, (cols, 1), 0)
    cells = [
        jnp.where(column < widths[r], latents_ref[r].astype(F32), 0.0) for r in range(row_count)
    ]
    write_stats(out_ref, cells, labels, widths, info.videos, channels)


def hidden_kernel(
    rows, info_ref, before_ref, latents_ref, after_ref, stats_ref, gain_ref, shift_ref, out_ref
):
    info = Info(info_ref, rows)
    row_count, cols, _ = latents_ref.shape
    labels, widths = info.window(info.tile() * row_count - 1, row_count + 2)
    means, scales = norm_tables(stats_ref, gain_ref)
    column = lax.broadcasted_iota(jnp.int32, (cols, 1), 0)
    for r in range(row_count + 2):
        if r == 0:
            source = before_ref[0]
        elif r == row_count + 1:
            source = after_ref[0]
        else:
            source = latents_ref[r - 1]
        mean = pick(means, labels[r], info.videos)
        scale = pick(scales, labels[r], info.videos)
        normed = (source.astype(F32) - mean) * scale + shift_ref[...]
        active = normed / (1.0 + jnp.exp(-normed))
        out_ref[r] = jnp.where(column < widths[r], active, 0.0).astype(BF16)


def conv_kernel(rows, taps, info_ref, *rest):
    hidden_refs, rest = rest[:taps], rest[taps:]
    weight_ref, latents_ref, bias_ref, own_ref, *rest = rest
    row_count, cols, channels = latents_ref.shape
    pair_refs, rest = rest[: row_count // 2], rest[row_count // 2 :]
    edge_ref, stats_ref, columns_ref, total_ref = rest
    info = Info(info_ref, rows)
    step = pl.program_id(0)
    tap = lax.rem(step, 3)
    near_rows = row_count + 2
    padded = columns_ref.shape[0] // near_rows
    labels, widths = info.window(info.tile() * row_count - 1, near_rows)

    for back, hidden_ref in enumerate(hidden_refs):

        @pl.when(step == 3 * back)
        def _():
            build_columns(
                columns_ref,
                [functools.partial(hidden_ref.__getitem__, r) for r in range(near_rows)],
            )

    start = pl.multiple_of(tap * padded, 16)
    product = jnp.dot(
        columns_ref[pl.ds(start, row_count * padded), :], weight_ref[0], preferred_element_type=F32
    )
    for r in range(row_count):
        lo, hi = r * padded, (r + 1) * padded
        near = jnp.where(tap == 0, labels[r], jnp.where(tap == 1, labels[r + 1], labels[r + 2]))
        part = jnp.where(near == labels[r + 1], product[lo:hi], 0.0)
        total_ref[lo:hi, :] = jnp.where(step == 0, part, total_ref[lo:hi, :] + part)

    @pl.when(step == 3 * taps - 1)
    def _():
        column = lax.broadcasted_iota(jnp.int32, (cols, 1), 0)
        cells = []
        for r in range(row_count):
            branch = total_ref[r * padded : r * padded + cols, :]
            value = latents_ref[r].astype(F32) + branch + bias_ref[...]
            value = jnp.where(column < widths[r + 1], value, 0.0).astype(BF16)
            cells.append(value.astype(F32))
        for pair, pair_ref in enumerate(pair_refs):
            both = jnp.concatenate(cells[2 * pair : 2 * pair + 2], axis=0).astype(BF16)
            own_ref[pair] = both
            pair_ref[0] = both
        odd = lax.rem(info.tile(), 2) == 1
        edge_ref[0] = jnp.where(odd, cells[-1], cells[0]).astype(BF16)
        write_stats(stats_ref, cells, labels[1:-1], widths[1:-1], info.videos, channels)


def split_rows(pairs_ref):
    cols = pairs_ref.shape[1] // 2
    cells = []
    for pair in range(pairs_ref.shape[0]):
        both = pairs_ref[pair].astype(F32)
        cells += [both[:cols], both[cols:]]
    return cells


def query_kernel(
    rows, info_ref, own_ref, other_ref, edge_ref, other_edge_ref, stats_ref, gain_ref, shift_ref,
    weight_ref, bias_ref, queries_ref, constant_ref,
):
    info = Info(info_ref, rows)
    pairs, double, channels = own_ref.shape
    cols = double // 2
    row_count = 2 * pairs
    odd = lax.rem(info.tile(), 2)
    labels, widths = info.window((info.tile() - odd) * row_count - 1, 2 * row_count + 2)
    means, scales = norm_tables(stats_ref, gain_ref)
    column = lax.broadcasted_iota(jnp.int32, (cols, 1), 0)
    own, other = split_rows(own_ref), split_rows(other_ref)
    edge, other_edge = edge_ref[0].astype(F32), other_edge_ref[0].astype(F32)
    even_order = [edge] + own + other + [other_edge]
    odd_order = [other_edge] + other + own + [edge]
    cells = []
    for r in range(2 * row_count + 2):
        values = jnp.where(odd == 1, odd_order[r], even_order[r])
        mean = pick(means, labels[r], info.videos)
        scale = pick(scales, labels[r], info.videos)
        normed = (values - mean) * scale + shift_ref[...]
        cells.append(jnp.where(column < widths[r], normed, 0.0))
    cells = jnp.concatenate(cells, axis=0).astype(BF16)
    queries = (
        jnp.dot(cells, weight_ref[:, 0:channels], preferred_element_type=F32)
        + bias_ref[:, 0:channels]
    ).astype(BF16)
    factor = channels ** (-0.5) * math.log2(math.e)
    turned = lax.dot_general(
        queries, weight_ref[:, channels : 2 * channels], (((1,), (1,)), ((), ())),
        preferred_element_type=F32,
    )
    queries_ref[...] = (turned * factor).astype(BF16)
    constant = jnp.sum(
        queries.astype(F32) * bias_ref[:, channels : 2 * channels], axis=1, keepdims=True
    )
    constant_ref[...] = jnp.broadcast_to(constant * factor, constant_ref.shape)


def attend_kernel(rows, chunk, chunks, info_ref, *rest):
    stats_ref, gain_ref, shift_ref, queries_ref, constant_ref, codes_ref, canvas_ref, *rest = rest
    first, last = chunk == 0, chunk == chunks - 1
    if not first:
        old_peak_ref, old_sum_ref, old_total_ref, *rest = rest
    out_refs, (keys_ref, total_ref) = rest[:3], rest[3:]
    info = Info(info_ref, rows)
    pairs, double, channels = canvas_ref.shape
    cols = double // 2
    block = codes_ref.shape[-1]
    per_block = block // double
    row_count = 2 * chunks
    cells = queries_ref.shape[0]
    odd = lax.rem(info.tile(), 2)
    first_row = (info.tile() - odd) * row_count
    labels = [info.label(first_row - 1 + r) for r in range(2 * row_count + 2)]
    lowest, highest = labels[1], labels[-2]
    means, scales = norm_tables(stats_ref, gain_ref)

    def pair_labels(pair):
        row = (2 * pair + odd) * row_count + 2 * chunk
        return [info.label(row), info.label(row + 1)]

    def count(pair, carried):
        below, upto = carried
        upper, lower = pair_labels(pair)
        return (
            below + (lower < lowest).astype(jnp.int32),
            upto + (upper <= highest).astype(jnp.int32),
        )

    first_pair, end_pair = lax.fori_loop(0, pairs, count, (jnp.int32(0), jnp.int32(0)))
    first_block = first_pair // per_block
    end_block = (end_pair + per_block - 1) // per_block

    def normalise(pair, carried):
        near = pair_labels(pair)
        both = canvas_ref[pair].astype(F32)
        halves = []
        for half in range(2):
            mean = pick(means, near[half], info.videos)
            scale = pick(scales, near[half], info.videos)
            halves.append((both[half * cols : (half + 1) * cols] - mean) * scale + shift_ref[...])
        start = pl.multiple_of(pair * double, 16)
        keys_ref[pl.ds(start, double), :] = jnp.concatenate(halves, axis=0).astype(BF16)
        return carried

    lax.fori_loop(first_block * per_block, end_block * per_block, normalise, jnp.int32(0))

    query_label = jnp.concatenate(
        [jnp.zeros((cols, 1), F32) + label.astype(F32) for label in labels], axis=0
    )
    constant = constant_ref[:, 0:1]
    if first:
        total_ref[...] = jnp.zeros(total_ref.shape, F32)
        state = (jnp.full((cells, 1), LOWEST, F32), jnp.zeros((cells, 1), F32))
    else:
        total_ref[...] = old_total_ref[...]
        state = (old_peak_ref[:, 0:1], old_sum_ref[:, 0:1])

    def step(index, carried):
        largest, denominator = carried
        start = pl.multiple_of(index * block, 16)
        keys = keys_ref[pl.ds(start, block), :]
        scores = lax.dot_general(
            queries_ref[...], keys, (((1,), (1,)), ((), ())), preferred_element_type=F32
        )
        scores = jnp.where(codes_ref[chunk, index] == query_label, scores, MASKED)
        peak = jnp.maximum(largest, jnp.max(scores, axis=1, keepdims=True) + constant)
        weights = jnp.exp2(scores - (peak - constant))
        factor = jnp.exp2(largest - peak)
        denominator = denominator * factor + jnp.sum(weights, axis=1, keepdims=True)
        total_ref[...] = total_ref[...] * factor + jnp.dot(
            weights.astype(BF16), keys, preferred_element_type=F32
        )
        return peak, denominator

    peak, denominator = lax.fori_loop(first_block, end_block, step, state)
    if not last:
        peak_ref, sum_ref, out_total_ref = out_refs
        peak_ref[...] = jnp.broadcast_to(peak, peak_ref.shape)
        sum_ref[...] = jnp.broadcast_to(denominator, sum_ref.shape)
        out_total_ref[...] = total_ref[...]
        return
    mean_ref, level_ref, sent_ref = out_refs
    some = denominator > 0.0
    safe = jnp.where(some, denominator, 1.0)
    total_ref[...] = total_ref[...] / safe
    level = jnp.where(some, peak + jnp.log2(safe), LOWEST)
    needed = row_count + 2
    span = row_count * cols
    mine = pl.multiple_of(odd * span, 16)
    yours = pl.multiple_of((1 - odd) * span, 16)
    mean_ref[...] = total_ref[pl.ds(mine, needed * cols), :]
    level_mine = jnp.where(odd == 1, level[span:], level[: needed * cols])
    level_yours = jnp.where(odd == 1, level[: needed * cols], level[span:])
    level_ref[...] = jnp.broadcast_to(level_mine, level_ref.shape)
    lane = lax.broadcasted_iota(jnp.int32, (cols, channels), 1)
    packed = jnp.zeros((cols, channels), F32)
    for r in range(needed):
        sent_ref[r] = total_ref[pl.ds(yours + r * cols, cols), :].astype(BF16)
        left = level_yours[r * cols : (r + 1) * cols]
        for part in range(3):
            rounded = left.astype(BF16).astype(F32)
            packed = jnp.where(lane == 3 * r + part, rounded, packed)
            left = left - rounded
    sent_ref[needed] = packed.astype(BF16)


def finish_kernel(
    rows, info_ref, mean_ref, level_ref, received_ref, own_ref, other_ref, edge_ref, triple_ref,
    triple_bias_ref, output_ref, output_bias_ref, weight_ref, bias_ref, out_ref, columns_ref,
    wide_ref,
):
    info = Info(info_ref, rows)
    pairs, double, channels = own_ref.shape
    cols = double // 2
    row_count = 2 * pairs
    near_rows = row_count + 2
    padded = columns_ref.shape[0] // near_rows
    parts_out = wide_ref.shape[0]
    out_channels = out_ref.shape[-1]
    odd = lax.rem(info.tile(), 2) == 1
    labels, widths = info.window(info.tile() * row_count - 1, near_rows)
    means = []
    levels = received_ref[near_rows].astype(F32)
    for r in range(near_rows):
        mine = level_ref[r * cols : (r + 1) * cols, 0:1]
        yours = (levels[:, 3 * r : 3 * r + 1] + levels[:, 3 * r + 1 : 3 * r + 2]) + levels[
            :, 3 * r + 2 : 3 * r + 3
        ]
        peak = jnp.maximum(mine, yours)
        weight, other_weight = jnp.exp2(mine - peak), jnp.exp2(yours - peak)
        share = weight / (weight + other_weight)
        received = received_ref[r].astype(F32)
        means.append(
            mean_ref[r * cols : (r + 1) * cols, :] * share + received * (1.0 - share)
        )
    mean_cell = jnp.concatenate(means, axis=0).astype(BF16)
    mixed = (
        jnp.dot(mean_cell, triple_ref[:, 2 * channels :], preferred_element_type=F32)
        + triple_bias_ref[:, 2 * channels :]
    ).astype(BF16)
    attended = jnp.dot(mixed, output_ref[...], preferred_element_type=F32) + output_bias_ref[...]
    own, other = split_rows(own_ref), split_rows(other_ref)
    edge = edge_ref[0].astype(F32)
    residual = (
        [jnp.where(odd, other[-1], edge)] + own + [jnp.where(odd, edge, other[0])]
    )
    column = lax.broadcasted_iota(jnp.int32, (cols, 1), 0)
    sources = []
    for r in range(near_rows):
        value = residual[r] + attended[r * cols : (r + 1) * cols]
        value = jnp.where(column < widths[r], value, 0.0).astype(BF16)
        sources.append(lambda value=value: value)
    build_columns(columns_ref, sources)
    span = row_count * padded
    wide_column = lax.broadcasted_iota(jnp.int32, (2 * cols, 1), 0)
    for down in range(2):
        for right in range(2):
            lanes = slice(right * channels, (right + 2) * channels)
            products = [
                jnp.dot(
                    columns_ref[(down + tap) * padded : (down + tap) * padded + span, lanes],
                    weight_ref[down, tap, right],
                    preferred_element_type=F32,
                )
                for tap in range(2)
            ]
            rim, same = products[down], products[1 - down]
            for r in range(row_count):
                lo, hi = r * padded, r * padded + cols
                near = labels[r + 2 * down]
                value = same[lo:hi] + jnp.where(near == labels[r + 1], rim[lo:hi], 0.0)
                for part in range(parts_out):
                    wide_ref[part, 2 * r + down, pl.ds(right, cols, 2), :] = value[
                        :, part * LANES : (part + 1) * LANES
                    ]
    for r in range(2 * row_count):
        valid = wide_column < 2 * widths[r // 2 + 1]
        for part in range(parts_out):
            lo, hi = part * LANES, min((part + 1) * LANES, out_channels)
            value = wide_ref[part, r, :, 0 : hi - lo] + bias_ref[:, lo:hi]
            out_ref[r, :, lo:hi] = jnp.where(valid, value, 0.0).astype(BF16)


def merge_stats(mine, other):
    count = mine[0] + other[0]
    safe = jnp.maximum(count, 1.0)
    off = other[1] - mine[1]
    mean = mine[1] + off * (other[0] / safe)
    spread = mine[2] + other[2] + off * off * (mine[0] * other[0] / safe)
    return jnp.stack([count, mean, spread])


def combined_weight(weight):
    wide = jnp.pad(weight.astype(F32), ((0, 0),) * 3 + ((0, -weight.shape[-1] % LANES),))
    rows = jnp.stack(
        [
            jnp.stack([wide[0], wide[1] + wide[2]]),
            jnp.stack([wide[0] + wide[1], wide[2]]),
        ]
    )
    left = jnp.concatenate([rows[:, :, 0], rows[:, :, 1] + rows[:, :, 2]], axis=2)
    right = jnp.concatenate([rows[:, :, 0] + rows[:, :, 1], rows[:, :, 2]], axis=2)
    return jnp.stack([left, right], axis=2).astype(BF16)


def shards(
    tiles,
    frames,
    latents,
    row_video,
    video_cols,
    first_gain,
    first_shift,
    conv_weight,
    conv_bias,
    second_gain,
    second_shift,
    triple_weight,
    triple_bias,
    output_weight,
    output_bias,
    upsample_weight,
    upsample_bias,
):
    row_count, frame_count, cols, channels = latents.shape
    assert frame_count == 1 and row_count == 2 * CHUNKS and tiles % 4 == 0
    out_channels = upsample_weight.shape[-1]
    rows = row_count * tiles
    cells = row_count * cols
    padded = -(-(cols + 1) // 16) * 16
    near_rows = row_count + 2
    halves = tiles // 2
    source = latents.reshape(row_count, cols, channels)
    tile = lax.axis_index("tile").astype(jnp.int32)
    info = jnp.concatenate([jnp.reshape(tile, (1,)), row_video, video_cols])

    def row(vector):
        return vector.reshape(1, -1)

    def shape(*dims, dtype=BF16):
        return jax.ShapeDtypeStruct(dims, dtype)

    def call(kernel, operands, out_shape, scratch=(), **kwargs):
        many = isinstance(out_shape, tuple)
        return pl.pallas_call(
            kernel,
            out_shape=out_shape,
            in_specs=[SMEM_SPEC] + [VMEM_SPEC] * len(operands),
            out_specs=(VMEM_SPEC,) * len(out_shape) if many else VMEM_SPEC,
            scratch_shapes=list(scratch),
            compiler_params=params(),
            **kwargs,
        )(info, *operands)

    before = lax.ppermute(source[row_count - 1 :], "tile", [(i, i + 1) for i in range(tiles - 1)])
    after = lax.ppermute(source[:1], "tile", [(i + 1, i) for i in range(tiles - 1)])
    stats_shape = shape(3, SLOTS, LANES, dtype=F32)
    stats = call(
        functools.partial(stats_kernel, rows), [source], stats_shape,
        cost_estimate=cost(cells * channels * 2, 2 * cells * channels), name="first_stats",
    )
    stats, before, after = lax.optimization_barrier((stats, before, after))

    def over_tiles(stats):
        bit = 1
        while bit < tiles:
            other = lax.ppermute(stats, "tile", [(i, i ^ bit) for i in range(tiles)])
            stats = merge_stats(stats, other)
            bit *= 2
        return stats

    stats = over_tiles(stats)
    hidden = call(
        functools.partial(hidden_kernel, rows),
        [before, source, after, stats, row(first_gain), row(first_shift)],
        shape(near_rows, cols, channels),
        cost_estimate=cost(cells * channels * 10, 5 * cells * channels, cells * channels),
        name="hidden",
    )

    taps = min(3, frames)
    context = [hidden] + [
        lax.ppermute(hidden, "frame", [(i, i + by) for i in range(frames - by)])
        for by in range(1, taps)
    ]

    def whole(*dims):
        return pl.BlockSpec(dims, lambda step: (0,) * len(dims))

    pair_dims = (1, 2 * cols, channels)
    own, *rest = pl.pallas_call(
        functools.partial(conv_kernel, rows, taps),
        grid=(3 * taps,),
        out_shape=(
            [shape(CHUNKS, 2 * cols, channels)]
            + [shape(*pair_dims)] * CHUNKS
            + [shape(1, cols, channels), stats_shape]
        ),
        in_specs=(
            [SMEM_SPEC]
            + [whole(near_rows, cols, channels)] * taps
            + [
                pl.BlockSpec(
                    (1, 3 * channels, channels),
                    lambda step: (3 * (2 - step // 3) + lax.rem(step, 3), 0, 0),
                ),
                whole(row_count, cols, channels),
                whole(1, channels),
            ]
        ),
        out_specs=(
            [whole(CHUNKS, 2 * cols, channels)]
            + [whole(*pair_dims)] * CHUNKS
            + [whole(1, cols, channels), whole(3, SLOTS, LANES)]
        ),
        scratch_shapes=[
            pltpu.VMEM((near_rows * padded, 3 * channels), BF16),
            pltpu.VMEM((row_count * padded, channels), F32),
        ],
        compiler_params=pltpu.CompilerParams(vmem_limit_bytes=CONV_VMEM_BYTES),
        cost_estimate=cost(
            9 * taps * cells * channels * channels, 18 * taps * channels * channels
        ),
        name="conv",
    )(info, *context, conv_weight.reshape(9, 3 * channels, channels), source, row(conv_bias))
    pieces, edge, stats = rest[:CHUNKS], rest[CHUNKS], rest[CHUNKS + 1]

    groups = [list(range(side, tiles, 2)) for side in range(2)]
    canvas = [
        lax.all_gather(piece, "tile", axis=0, tiled=True, axis_index_groups=groups)
        for piece in pieces
    ]
    neighbour = [(i, i ^ 1) for i in range(tiles)]
    outer = [(i, i - 1 if i % 2 == 0 else i + 1) for i in range(tiles)]
    outer = [(i, j) for i, j in outer if 0 <= j < tiles]
    stats = over_tiles(stats)
    far_edge = lax.ppermute(edge, "tile", outer)
    other = lax.ppermute(own, "tile", neighbour)
    other_edge = lax.ppermute(far_edge, "tile", neighbour)
    gain, shift = row(second_gain), row(second_shift)
    query_cells = (2 * row_count + 2) * cols
    queries, constant = call(
        functools.partial(query_kernel, rows),
        [
            own, other, far_edge, other_edge, stats, gain, shift, triple_weight, row(triple_bias)
        ],
        (shape(query_cells, channels), shape(query_cells, LANES, dtype=F32)),
        cost_estimate=cost(2 * query_cells * channels * channels, 4 * query_cells * channels),
        name="queries",
    )
    widths = jnp.sum(
        jnp.where(
            row_video[:, None] == jnp.arange(video_cols.shape[0], dtype=jnp.int32)[None, :],
            video_cols[None, :],
            0,
        ),
        axis=1,
    )
    valid = jnp.arange(cols, dtype=jnp.int32)[None, :] < widths[:, None]
    codes = jnp.where(valid, row_video[:, None], -2).astype(F32)
    codes = codes.reshape(halves, 2, CHUNKS, 2 * cols)
    codes = lax.dynamic_index_in_dim(codes, tile % 2, axis=1, keepdims=False)
    codes = jnp.transpose(codes, (1, 0, 2)).reshape(CHUNKS, halves // 2, 1, 4 * cols)
    state = []
    for chunk in range(CHUNKS):
        last = chunk == CHUNKS - 1
        if last:
            outs = (
                shape(near_rows * cols, channels, dtype=F32),
                shape(near_rows * cols, LANES, dtype=F32),
                shape(near_rows + 1, cols, channels),
            )
        else:
            outs = (
                shape(query_cells, LANES, dtype=F32),
                shape(query_cells, LANES, dtype=F32),
                shape(query_cells, channels, dtype=F32),
            )
        keys = halves * 2 * cols
        state = call(
            functools.partial(attend_kernel, rows, chunk, CHUNKS),
            [stats, gain, shift, queries, constant, codes, canvas[chunk], *state],
            outs,
            scratch=[
                pltpu.VMEM((keys, channels), BF16),
                pltpu.VMEM((query_cells, channels), F32),
            ],
            cost_estimate=cost(
                2 * query_cells * keys * channels, 2 * keys * channels, query_cells * keys
            ),
            name="attend_last" if last else "attend_part",
        )
    mean, level, sent = state

    received = lax.ppermute(sent, "tile", neighbour)
    decoded = call(
        functools.partial(finish_kernel, rows),
        [
            mean, level, received, own, other, far_edge, triple_weight, row(triple_bias),
            output_weight, row(output_bias), combined_weight(upsample_weight), row(upsample_bias),
        ],
        shape(2 * row_count, 2 * cols, out_channels),
        scratch=[
            pltpu.VMEM((near_rows * padded, 3 * channels), BF16),
            pltpu.VMEM((-(-out_channels // LANES), 2 * row_count, 2 * cols, LANES), F32),
        ],
        cost_estimate=cost(16 * cells * channels * out_channels, 8 * cells * out_channels),
        name="finish",
    )
    return decoded.reshape(2 * row_count, 1, 2 * cols, out_channels)


def solution(mesh):
    sizes = dict(mesh.shape)
    in_specs = (P("tile", "frame", None, None),) + (P(),) * 14
    out_specs = P("tile", "frame", None, None)
    body = functools.partial(shards, sizes["tile"], sizes["frame"])
    return jax.shard_map(body, mesh=mesh, in_specs=in_specs, out_specs=out_specs, check_vma=False)
```

time: 155 us -> 178 us (1.15)
  the two profiles are of different devices: /device:TPU:17 before, /device:TPU:8 now
where the time goes in v2:
time: 178 us; the launch traced here: 176 us
  waiting for transfers between devices  67 us (38%)
  Pallas kernels  39 us (22%)
  starting transfers between devices  27.2 us (15%)
  local copies, waits for them, and re-layouts  18.9 us (11%)
  between operations  13.9 us (8%)
  other arithmetic  9.8 us (6%)
    all_gather x2, waiting for transfers between devices, shards(): lax.all_gather(piece, 'tile', axis=0, tiled=True, axis_index_groups=groups)  32.7 us
    pallas_call x6, Pallas kernels, call(): pl.pallas_call(kernel, out_shape=out_shape, in_specs=[SMEM_SPEC] + [VMEM_...  29 us
    unnamed x67, local copies, waits for them, and re-layouts  14 us
    ppermute x8, waiting for transfers between devices, over_tiles(): other = lax.ppermute(stats, 'tile', [(i, i ^ bit) for i in range(tiles)])  13.8 us
    ppermute x8, starting transfers between devices, over_tiles(): other = lax.ppermute(stats, 'tile', [(i, i ^ bit) for i in range(tiles)])  11 us
    ppermute x1, waiting for transfers between devices, shards(): received = lax.ppermute(sent, 'tile', neighbour)  10.1 us
    pallas_call x1, Pallas kernels, shards(): pl.pallas_call(functools.partial(conv_kernel, rows, taps), grid=(3 * taps...  10 us
    ppermute x1, waiting for transfers between devices, shards(): far_edge = lax.ppermute(edge, 'tile', outer)  5.01 us
  transfers between devices with their start and end apart: 17, of which 12 were waited for; matrix products, arithmetic and copies ran while one was open for 8% of the time, Pallas kernels for 8%

profile of v2, /device:TPU:8, one launch (start us, length us, event | category | flops | bytes accessed | tf_op | source)
XLA Modules:
  0.0 175.8 jit_solution(14427369514081250402)
XLA Ops:
  7.5 3.4 %collective-permute-start = (bf16[1,104,384]{2,1,0:T(8,128)(2,1)S(1)}, bf16[1,104,384]{2,1,0:T(8,128)(2,1)S(1)}, u32[]{:S(2)}, u32[]{:S(2)}) collective-permute-start(bf16[1,104,384]{2,1,0:T(8,128)(2,1)S(1)} %get-tuple-element.62), channel_id=1, source_target_pairs={{0,2},{2,4},{4,6},{6,8},{8,10},{10,12},{12,14},{14,16},{16,18},{18... | collective-permute-start | bytes 239624 | tf_op jit(solution)/shard_map/ppermute | solution.py:530
  10.9 4.2 %collective-permute-start.1 = (bf16[1,104,384]{2,1,0:T(8,128)(2,1)S(1)}, bf16[1,104,384]{2,1,0:T(8,128)(2,1)S(1)}, u32[]{:S(2)}, u32[]{:S(2)}) collective-permute-start(bf16[1,104,384]{2,1,0:T(8,128)(2,1)S(1)} %get-tuple-element.61), channel_id=1, source_target_pairs={{2,0},{4,2},{6,4},{8,6},{10,8},{12,10},{14,12},{16,14},{18,16},{20... | collective-permute-start | bytes 239624 | tf_op jit(solution)/shard_map/ppermute | solution.py:531
  16.9 1.8 %first_stats.1 = f32[3,8,128]{2,1,0:T(8,128)S(1)} custom-call(s32[67]{0:T(128)S(1)} %pad_add_fusion.info_ref, bf16[4,104,384]{2,1,0:T(8,128)(2,1)S(1)} %bitcast.38), custom_call_target="tpu_custom_call" | custom-call | flops 638976 | bytes 319488 | tf_op jit(solution)/shard_map/first_stats/pallas_call | solution.py:520
  19.6 2.9 %collective-permute-done.2 = f32[3,8,128]{2,1,0:T(8,128)S(1)} collective-permute-done((f32[3,8,128]{2,1,0:T(8,128)S(1)}, f32[3,8,128]{2,1,0:T(8,128)S(1)}, u32[]{:S(2)}, u32[]{:S(2)}) %collective-permute-start.2) | collective-permute-done | bytes 12320 | tf_op jit(solution)/shard_map/ppermute | solution.py:542
  23.8 2.5 %collective-permute-done.3 = f32[3,8,128]{2,1,0:T(8,128)S(1)} collective-permute-done((f32[3,8,128]{2,1,0:T(8,128)S(1)}, f32[3,8,128]{2,1,0:T(8,128)S(1)}, u32[]{:S(2)}, u32[]{:S(2)}) %collective-permute-start.3) | collective-permute-done | bytes 12320 | tf_op jit(solution)/shard_map/ppermute | solution.py:542
  26.4 3.7 %collective-permute-done.4 = f32[3,8,128]{2,1,0:T(8,128)S(1)} collective-permute-done((f32[3,8,128]{2,1,0:T(8,128)S(1)}, f32[3,8,128]{2,1,0:T(8,128)S(1)}, u32[]{:S(2)}, u32[]{:S(2)}) %collective-permute-start.4) | collective-permute-done | bytes 12320 | tf_op jit(solution)/shard_map/ppermute | solution.py:542
  30.1 2.7 %collective-permute-start.5 = (f32[3,8,128]{2,1,0:T(8,128)S(1)}, f32[3,8,128]{2,1,0:T(8,128)S(1)}, u32[]{:S(2)}, u32[]{:S(2)}) collective-permute-start(f32[3,8,128]{2,1,0:T(8,128)S(1)} %pad_maximum_fusion.4), channel_id=1, source_target_pairs={{0,16},{2,18},{4,20},{6,22},{8,24},{10,26},{12,28},{14,30},{16,0},... | collective-permute-start | bytes 36872 | tf_op jit(solution)/shard_map/ppermute | solution.py:542
  39.7 10.0 %conv.1 = (bf16[2,208,384]{2,1,0:T(8,128)(2,1)}, bf16[1,208,384]{2,1,0:T(8,128)(2,1)}, bf16[1,208,384]{2,1,0:T(8,128)(2,1)}, bf16[1,104,384]{2,1,0:T(8,128)(2,1)}, f32[3,8,128]{2,1,0:T(8,128)}) custom-call(s32[67]{0:T(128)} %copy-done.5, bf16[6,104,384]{2,1,0:T(8,128)(2,1)} %copy-done.1, bf16[6,104,384]{2,1,0:T(8,128)(2,1)} %copy-done.23, ...), custom_call_target="tpu_custom_call" | custom-call | flops 2208301056 | bytes 5308416 | tf_op jit(solution)/shard_map/conv/pallas_call | solution.py:566
  52.9 2.8 %maximum_bitcast_fusion = (f32[1,2,3,384,256]{4,3,1,0,2:T(8,128)}, f32[1,2,3,384,256]{4,3,1,0,2:T(8,128)}) fusion(f32[1,3,384,256]{3,2,0,1:T(8,128)S(1)} %get-tuple-element.60, f32[1,3,384,256]{3,2,0,1:T(8,128)S(1)} %get-tuple-element.57, f32[1,3,384,256]{3,2,0,1:T(8,128)S(1)} %get-tuple-element.59, f32[1,3,384,256]{3,2,0,1:T(8,128)S(1)} %get-tuple-element.58), kind=kLoop, calls=%fused_computation.5 | loop fusion | flops 1179648 | bytes 9437184 | tf_op jit(solution)/shard_map/stack | solution.py:470
  55.8 2.1 %collective-permute-start.8 = (f32[3,8,128]{2,1,0:T(8,128)S(1)}, f32[3,8,128]{2,1,0:T(8,128)S(1)}, u32[]{:S(2)}, u32[]{:S(2)}) collective-permute-start(f32[3,8,128]{2,1,0:T(8,128)S(1)} %pad_maximum_fusion.6), channel_id=1, source_target_pairs={{0,4},{2,6},{4,0},{6,2},{8,12},{10,14},{12,8},{14,10},{16,20},{18,... | collective-permute-start | bytes 36872 | tf_op jit(solution)/shard_map/ppermute | solution.py:542
  60.1 3.2 %collective-permute-done.9 = f32[3,8,128]{2,1,0:T(8,128)S(1)} collective-permute-done((f32[3,8,128]{2,1,0:T(8,128)S(1)}, f32[3,8,128]{2,1,0:T(8,128)S(1)}, u32[]{:S(2)}, u32[]{:S(2)}) %collective-permute-start.9) | collective-permute-done | bytes 12320 | tf_op jit(solution)/shard_map/ppermute | solution.py:542
  63.3 2.4 %collective-permute-start.10 = (f32[3,8,128]{2,1,0:T(8,128)S(1)}, f32[3,8,128]{2,1,0:T(8,128)S(1)}, u32[]{:S(2)}, u32[]{:S(2)}) collective-permute-start(f32[3,8,128]{2,1,0:T(8,128)S(1)} %pad_maximum_fusion.8), channel_id=1, source_target_pairs={{0,16},{2,18},{4,20},{6,22},{8,24},{10,26},{12,28},{14,30},{16,0},... | collective-permute-start | bytes 36872 | tf_op jit(solution)/shard_map/ppermute | solution.py:542
  65.8 4.5 %fusion.2 = (bf16[2,2,384,256]{3,2,1,0:T(8,128)(2,1)}, bf16[2,2,384,256]{3,2,1,0:T(8,128)(2,1)}) fusion(f32[1,2,3,384,256]{4,3,1,0,2:T(8,128)} %get-tuple-element.64, f32[1,2,3,384,256]{4,3,1,0,2:T(8,128)} %get-tuple-element.63), kind=kLoop, calls=%fused_computation.17 | loop fusion | flops 3145728 | bytes 6291456 | tf_op jit(solution)/shard_map/convert.9
  71.6 4.5 %collective-permute-start.12 = (bf16[1,104,384]{2,1,0:T(8,128)(2,1)S(1)}, bf16[1,104,384]{2,1,0:T(8,128)(2,1)S(1)}, u32[]{:S(2)}, u32[]{:S(2)}) collective-permute-start(bf16[1,104,384]{2,1,0:T(8,128)(2,1)S(1)} %copy-done.32), channel_id=1, source_target_pairs={{2,4},{4,2},{6,8},{8,6},{10,12},{12,10},{14,16},{16,14},{18,20},{2... | collective-permute-start | bytes 239624 | tf_op jit(solution)/shard_map/ppermute | solution.py:612
  76.1 5.0 %collective-permute-done.12.edge_ref = bf16[1,104,384]{2,1,0:T(8,128)(2,1)S(1)} collective-permute-done((bf16[1,104,384]{2,1,0:T(8,128)(2,1)S(1)}, bf16[1,104,384]{2,1,0:T(8,128)(2,1)S(1)}, u32[]{:S(2)}, u32[]{:S(2)}) %collective-permute-start.12) | collective-permute-done | bytes 79904 | tf_op jit(solution)/shard_map/ppermute | solution.py:612
  81.2 4.4 %collective-permute-done.13.other_edge_ref = bf16[1,104,384]{2,1,0:T(8,128)(2,1)S(1)} collective-permute-done((bf16[1,104,384]{2,1,0:T(8,128)(2,1)S(1)}, bf16[1,104,384]{2,1,0:T(8,128)(2,1)S(1)}, u32[]{:S(2)}, u32[]{:S(2)}) %collective-permute-start.13) | collective-permute-done | bytes 79904 | tf_op jit(solution)/shard_map/ppermute | solution.py:614
  85.6 2.3 %queries.1 = (bf16[1040,384]{1,0:T(8,128)(2,1)S(1)}, f32[1040,128]{1,0:T(8,128)S(1)}) custom-call(s32[67]{0:T(128)S(1)} %copy-done.6, bf16[2,208,384]{2,1,0:T(8,128)(2,1)S(1)} %copy-done.3, bf16[2,208,384]{2,1,0:T(8,128)(2,1)S(1)} %collective-permute-done.11.other_ref, bf16[1,104,384]{2,1,0:T(8,128)(2,1)S(1)} %collective-permute-done.12.edge_ref, ...), custom_call_target="tpu_custom_call" | custom-call | flops 613416960 | bytes 1597440 | tf_op jit(solution)/shard_map/queries/pallas_call | solution.py:520
  87.9 4.3 %all-gather.5.cloned.1.call-done.rest_6_ = bf16[8,208,384]{2,1,0:T(8,128)(2,1)} async-done(((bf16[1,208,384]{2,1,0:T(8,128)(2,1)}), bf16[8,208,384]{2,1,0:T(8,128)(2,1)}) %all-gather.5.cloned.1.call-update) | async-done | bytes 1277968 | tf_op jit(solution)/shard_map/all_gather | solution.py:605
  93.5 9.9 %attend_part.1 = (f32[1040,128]{1,0:T(8,128)S(1)}, f32[1040,128]{1,0:T(8,128)S(1)}, f32[1040,384]{1,0:T(8,128)S(1)}) custom-call(s32[67]{0:T(128)S(1)} %copy-done.6, f32[3,8,128]{2,1,0:T(8,128)S(1)} %pad_maximum_fusion.9.stats_ref.rest_0_, f32[1,384]{1,0:T(1,128)S(1)} %reshape.58.gain_ref.rest_1_, f32[1,384]{1,0:T(1,128)S(1)} %reshape.59.shift_ref.rest_2_, ...), custom_call_target="tpu_custom_call" | custom-call | flops 2658140160 | bytes 1277952 | tf_op jit(solution)/shard_map/attend_part/pallas_call | solution.py:520
  106.2 28.4 %all-gather.3.cloned.1.call-done.rest_6_ = bf16[8,208,384]{2,1,0:T(8,128)(2,1)} async-done(((bf16[1,208,384]{2,1,0:T(8,128)(2,1)}), bf16[8,208,384]{2,1,0:T(8,128)(2,1)}) %all-gather.3.cloned.1.call-update) | async-done | bytes 1277968 | tf_op jit(solution)/shard_map/all_gather | solution.py:605
  140.5 10.0 %attend_last.1 = (f32[624,384]{1,0:T(8,128)S(1)}, f32[624,128]{1,0:T(8,128)S(1)}, bf16[7,104,384]{2,1,0:T(8,128)(2,1)S(1)}) custom-call(s32[67]{0:T(128)S(1)} %copy-done.6, f32[3,8,128]{2,1,0:T(8,128)S(1)} %pad_maximum_fusion.9.stats_ref.rest_0_, f32[1,384]{1,0:T(1,128)S(1)} %reshape.58.gain_ref.rest_1_, f32[1,384]{1,0:T(1,128)S(1)} %reshape.59.shift_ref.rest_2_, ...), custom_call_target="tpu_custom_call" | custom-call | flops 2658140160 | bytes 1277952 | tf_op jit(solution)/shard_map/attend_last/pallas_call | solution.py:520
  150.5 1.5 collective-permute-start.14
  154.0 10.1 %collective-permute-done.14.received_ref = bf16[7,104,384]{2,1,0:T(8,128)(2,1)S(1)} collective-permute-done((bf16[7,104,384]{2,1,0:T(8,128)(2,1)S(1)}, bf16[7,104,384]{2,1,0:T(8,128)(2,1)S(1)}, u32[]{:S(2)}, u32[]{:S(2)}) %collective-permute-start.14) | collective-permute-done | bytes 559136 | tf_op jit(solution)/shard_map/ppermute | solution.py:670
  164.1 3.6 %finish.1 = bf16[8,208,192]{2,1,0:T(8,128)(2,1)S(1)} custom-call(s32[67]{0:T(128)S(1)} %copy-done.6, f32[624,384]{1,0:T(8,128)S(1)} %get-tuple-element.34.mean_ref, f32[624,128]{1,0:T(8,128)S(1)} %get-tuple-element.35.level_ref, bf16[7,104,384]{2,1,0:T(8,128)(2,1)S(1)} %collective-permute-done.14.received_ref, bf16[2,208,384]{2,1,0:T(8,128)(2,1)S(1)} %copy-done.3, ...), custom_call_target="tpu_custom_call" | custom-call | flops 981467136 | bytes 638976 | tf_op jit(solution)/shard_map/finish/pallas_call | solution.py:520
  (141 shorter events, 31.6 us)
Async XLA Ops:
  6.5 30.9 %copy-start.26 = (f32[384]{0:T(512)S(1)}, f32[384]{0:T(512)}, u32[]{:S(2)}) copy-start(f32[384]{0:T(512)} %param.21) | copy-start | bytes 4612
  6.5 85.7 %all-gather.5.cloned.1.call-start = ((), (), s32[]{:S(2)}) async-start(), calls=%async_computation.1 | async-start | bytes 1437696 | tf_op jit(solution)/shard_map/all_gather | solution.py:605
  7.5 11.2 %collective-permute-start = (bf16[1,104,384]{2,1,0:T(8,128)(2,1)S(1)}, bf16[1,104,384]{2,1,0:T(8,128)(2,1)S(1)}, u32[]{:S(2)}, u32[]{:S(2)}) collective-permute-start(bf16[1,104,384]{2,1,0:T(8,128)(2,1)S(1)} %get-tuple-element.62), channel_id=1, source_target_pairs={{0,2},{2,4},{4,6},{6,8},{8,10},{10,12},{12,14},{14,16},{16,18},{18... | collective-permute-start | bytes 239624 | tf_op jit(solution)/shard_map/ppermute | solution.py:530
  10.9 7.8 %collective-permute-start.1 = (bf16[1,104,384]{2,1,0:T(8,128)(2,1)S(1)}, bf16[1,104,384]{2,1,0:T(8,128)(2,1)S(1)}, u32[]{:S(2)}, u32[]{:S(2)}) collective-permute-start(bf16[1,104,384]{2,1,0:T(8,128)(2,1)S(1)} %get-tuple-element.61), channel_id=1, source_target_pairs={{2,0},{4,2},{6,4},{8,6},{10,8},{12,10},{14,12},{16,14},{18,16},{20... | collective-permute-start | bytes 239624 | tf_op jit(solution)/shard_map/ppermute | solution.py:531
  15.9 23.0 %copy-start.5 = (s32[67]{0:T(128)}, s32[67]{0:T(128)S(1)}, u32[]{:S(2)}) copy-start(s32[67]{0:T(128)S(1)} %pad_add_fusion.info_ref) | copy-start | bytes 808
  18.7 3.8 %collective-permute-start.2 = (f32[3,8,128]{2,1,0:T(8,128)S(1)}, f32[3,8,128]{2,1,0:T(8,128)S(1)}, u32[]{:S(2)}, u32[]{:S(2)}) collective-permute-start(f32[3,8,128]{2,1,0:T(8,128)S(1)} %first_stats.1), channel_id=1, source_target_pairs={{0,2},{2,0},{4,6},{6,4},{8,10},{10,8},{12,14},{14,12},{16,18},{18,... | collective-permute-start | bytes 36872 | tf_op jit(solution)/shard_map/ppermute | solution.py:542
  22.5 3.8 %collective-permute-start.3 = (f32[3,8,128]{2,1,0:T(8,128)S(1)}, f32[3,8,128]{2,1,0:T(8,128)S(1)}, u32[]{:S(2)}, u32[]{:S(2)}) collective-permute-start(f32[3,8,128]{2,1,0:T(8,128)S(1)} %pad_maximum_fusion.2), channel_id=1, source_target_pairs={{0,4},{2,6},{4,0},{6,2},{8,12},{10,14},{12,8},{14,10},{16,20},{18,... | collective-permute-start | bytes 36872 | tf_op jit(solution)/shard_map/ppermute | solution.py:542
  26.3 3.8 %collective-permute-start.4 = (f32[3,8,128]{2,1,0:T(8,128)S(1)}, f32[3,8,128]{2,1,0:T(8,128)S(1)}, u32[]{:S(2)}, u32[]{:S(2)}) collective-permute-start(f32[3,8,128]{2,1,0:T(8,128)S(1)} %pad_maximum_fusion.3), channel_id=1, source_target_pairs={{0,8},{2,10},{4,12},{6,14},{8,0},{10,2},{12,4},{14,6},{16,24},{18,... | collective-permute-start | bytes 36872 | tf_op jit(solution)/shard_map/ppermute | solution.py:542
  30.1 4.7 %collective-permute-start.5 = (f32[3,8,128]{2,1,0:T(8,128)S(1)}, f32[3,8,128]{2,1,0:T(8,128)S(1)}, u32[]{:S(2)}, u32[]{:S(2)}) collective-permute-start(f32[3,8,128]{2,1,0:T(8,128)S(1)} %pad_maximum_fusion.4), channel_id=1, source_target_pairs={{0,16},{2,18},{4,20},{6,22},{8,24},{10,26},{12,28},{14,30},{16,0},... | collective-permute-start | bytes 36872 | tf_op jit(solution)/shard_map/ppermute | solution.py:542
  36.1 2.8 %collective-permute-start.6 = (bf16[6,104,384]{2,1,0:T(8,128)(2,1)S(1)}, bf16[6,104,384]{2,1,0:T(8,128)(2,1)S(1)}, u32[]{:S(2)}, u32[]{:S(2)}) collective-permute-start(bf16[6,104,384]{2,1,0:T(8,128)(2,1)S(1)} %hidden.1.rest_0_), channel_id=1, source_target_pairs={{0,1},{2,3},{4,5},{6,7},{8,9},{10,11},{12,13},{14,15},{16,17},{18,... | collective-permute-start | bytes 1437704 | tf_op jit(solution)/shard_map/ppermute | solution.py:558
  49.7 84.9 %all-gather.3.cloned.1.call-start = ((), (), s32[]{:S(2)}) async-start(), calls=%async_computation | async-start | bytes 1437696 | tf_op jit(solution)/shard_map/all_gather | solution.py:605
  51.7 4.0 %collective-permute-start.7 = (f32[3,8,128]{2,1,0:T(8,128)S(1)}, f32[3,8,128]{2,1,0:T(8,128)S(1)}, u32[]{:S(2)}, u32[]{:S(2)}) collective-permute-start(f32[3,8,128]{2,1,0:T(8,128)S(1)} %copy-done.24), channel_id=1, source_target_pairs={{0,2},{2,0},{4,6},{6,4},{8,10},{10,8},{12,14},{14,12},{16,18},{18,... | collective-permute-start | bytes 36872 | tf_op jit(solution)/shard_map/ppermute | solution.py:542
  55.8 3.8 %collective-permute-start.8 = (f32[3,8,128]{2,1,0:T(8,128)S(1)}, f32[3,8,128]{2,1,0:T(8,128)S(1)}, u32[]{:S(2)}, u32[]{:S(2)}) collective-permute-start(f32[3,8,128]{2,1,0:T(8,128)S(1)} %pad_maximum_fusion.6), channel_id=1, source_target_pairs={{0,4},{2,6},{4,0},{6,2},{8,12},{10,14},{12,8},{14,10},{16,20},{18,... | collective-permute-start | bytes 36872 | tf_op jit(solution)/shard_map/ppermute | solution.py:542
  59.6 3.8 %collective-permute-start.9 = (f32[3,8,128]{2,1,0:T(8,128)S(1)}, f32[3,8,128]{2,1,0:T(8,128)S(1)}, u32[]{:S(2)}, u32[]{:S(2)}) collective-permute-start(f32[3,8,128]{2,1,0:T(8,128)S(1)} %pad_maximum_fusion.7), channel_id=1, source_target_pairs={{0,8},{2,10},{4,12},{6,14},{8,0},{10,2},{12,4},{14,6},{16,24},{18,... | collective-permute-start | bytes 36872 | tf_op jit(solution)/shard_map/ppermute | solution.py:542
  63.3 12.7 %collective-permute-start.10 = (f32[3,8,128]{2,1,0:T(8,128)S(1)}, f32[3,8,128]{2,1,0:T(8,128)S(1)}, u32[]{:S(2)}, u32[]{:S(2)}) collective-permute-start(f32[3,8,128]{2,1,0:T(8,128)S(1)} %pad_maximum_fusion.8), channel_id=1, source_target_pairs={{0,16},{2,18},{4,20},{6,22},{8,24},{10,26},{12,28},{14,30},{16,0},... | collective-permute-start | bytes 36872 | tf_op jit(solution)/shard_map/ppermute | solution.py:542
  65.8 19.8 %copy-start.2 = (bf16[384,1152]{1,0:T(8,128)(2,1)S(1)}, bf16[384,1152]{1,0:T(8,128)(2,1)}, u32[]{:S(2)}) copy-start(bf16[384,1152]{1,0:T(8,128)(2,1)} %triple_ref.1) | copy-start | bytes 2654212
  65.8 19.8 %copy-start.6 = (s32[67]{0:T(128)S(1)}, s32[67]{0:T(128)}, u32[]{:S(2)}) copy-start(s32[67]{0:T(128)} %copy-done.5) | copy-start | bytes 808
  70.4 15.1 %collective-permute-start.11 = (bf16[2,208,384]{2,1,0:T(8,128)(2,1)S(1)}, bf16[2,208,384]{2,1,0:T(8,128)(2,1)S(1)}, u32[]{:S(2)}, u32[]{:S(2)}) collective-permute-start(bf16[2,208,384]{2,1,0:T(8,128)(2,1)S(1)} %copy-done.3), channel_id=1, source_target_pairs={{0,2},{2,0},{4,6},{6,4},{8,10},{10,8},{12,14},{14,12},{16,18},{18,... | collective-permute-start | bytes 958472 | tf_op jit(solution)/shard_map/ppermute | solution.py:613
  71.6 9.5 %collective-permute-start.12 = (bf16[1,104,384]{2,1,0:T(8,128)(2,1)S(1)}, bf16[1,104,384]{2,1,0:T(8,128)(2,1)S(1)}, u32[]{:S(2)}, u32[]{:S(2)}) collective-permute-start(bf16[1,104,384]{2,1,0:T(8,128)(2,1)S(1)} %copy-done.32), channel_id=1, source_target_pairs={{2,4},{4,2},{6,8},{8,6},{10,12},{12,10},{14,16},{16,14},{18,20},{2... | collective-permute-start | bytes 239624 | tf_op jit(solution)/shard_map/ppermute | solution.py:612
  81.1 4.4 %collective-permute-start.13 = (bf16[1,104,384]{2,1,0:T(8,128)(2,1)S(1)}, bf16[1,104,384]{2,1,0:T(8,128)(2,1)S(1)}, u32[]{:S(2)}, u32[]{:S(2)}) collective-permute-start(bf16[1,104,384]{2,1,0:T(8,128)(2,1)S(1)} %collective-permute-done.12.edge_ref), channel_id=1, source_target_pairs={{0,2},{2,0},{4,6},{6,4},{8,10},{10,8},{12,14},{14,12},{16,18},{18,... | collective-permute-start | bytes 239624 | tf_op jit(solution)/shard_map/ppermute | solution.py:614
  87.9 15.5 %copy-start.10 = (f32[1040,128]{1,0:T(8,128)}, f32[1040,128]{1,0:T(8,128)S(1)}, u32[]{:S(2)}) copy-start(f32[1040,128]{1,0:T(8,128)S(1)} %get-tuple-element.28.rest_4_) | copy-start | bytes 1597444
  140.5 11.6 %copy-start.18 = (f32[1,2,3,384,256]{4,3,1,0,2:T(8,128)S(1)}, f32[1,2,3,384,256]{4,3,1,0,2:T(8,128)}, u32[]{:S(2)}) copy-start(f32[1,2,3,384,256]{4,3,1,0,2:T(8,128)} %get-tuple-element.63) | copy-start | bytes 7077892
  140.5 11.6 %copy-start.19 = (f32[1,2,3,384,256]{4,3,1,0,2:T(8,128)S(1)}, f32[1,2,3,384,256]{4,3,1,0,2:T(8,128)}, u32[]{:S(2)}) copy-start(f32[1,2,3,384,256]{4,3,1,0,2:T(8,128)} %get-tuple-element.64) | copy-start | bytes 7077892
  150.5 13.6 %collective-permute-start.14 = (bf16[7,104,384]{2,1,0:T(8,128)(2,1)S(1)}, bf16[7,104,384]{2,1,0:T(8,128)(2,1)S(1)}, u32[]{:S(2)}, u32[]{:S(2)}) collective-permute-start(bf16[7,104,384]{2,1,0:T(8,128)(2,1)S(1)} %get-tuple-element.36), channel_id=1, source_target_pairs={{0,2},{2,0},{4,6},{6,4},{8,10},{10,8},{12,14},{14,12},{16,18},{18,... | collective-permute-start | bytes 1677320 | tf_op jit(solution)/shard_map/ppermute | solution.py:670
  (26 other events, 85.1 us)
Sparse Core Ops, SparseCore 0:
  49.8 42.3 all-gather.4
  94.4 40.1 all-gather.2
